TPU v7x, 32 devices: a whole 2x2x4 slice. The times are simulated.
32 devices in a mesh: src: 8 (over y, x, core), rcv: 4 (over z).
Axes of the slice: x: 2, y: 2, z: 4, core: 2. Of those that a mesh axis runs over, the one named last changes fastest.
Arguments:
- data: bfloat16 [2, 6144, 6144], P(None, 'src', 'rcv'), may hold values from -24 to 24
- source_term: float32 [2, 6144], P(None, 'src'), may hold values from -1 to 1
Outputs:
- matched: bfloat16 [2, 6144, 6144], P(None, 'src', 'rcv')
All inputs are finite; a program needn't handle non-finite values.
Results may differ from a plain program's by a relative error of at most 0.0057.
Values may be sent and summed in bfloat16 or wider, within the bound.
A program may use at most 128 MiB of HBM per device.

v0:
```python
import jax
import jax.numpy as jnp
from jax import lax
from jax.sharding import PartitionSpec as P

LINE = 64


stabiliser = 1e-05


def with_halo(block, sides, width):
    for axis, dim in sides:
        count = lax.axis_size(axis)
        forward = [(i, i + 1) for i in range(count - 1)]
        backward = [(target, source) for source, target in forward]
        low = lax.ppermute(
            lax.slice_in_dim(block, block.shape[dim] - width, None, axis=dim), axis, forward
        )
        high = lax.ppermute(lax.slice_in_dim(block, 0, width, axis=dim), axis, backward)
        block = jnp.concatenate([low, block, high], axis=dim)
    return block


def complex_product(left_part, right_part):
    real_part = jnp.dot(left_part[0], right_part[0], preferred_element_type=jnp.float32) - jnp.dot(
        left_part[1], right_part[1], preferred_element_type=jnp.float32
    )
    imag_part = jnp.dot(left_part[0], right_part[1], preferred_element_type=jnp.float32) + jnp.dot(
        left_part[1], right_part[0], preferred_element_type=jnp.float32
    )
    return jnp.stack([real_part, imag_part])


def line_block_sums(multiples, data):
    mult = multiples.astype(jnp.float32)
    recorded = data.astype(jnp.float32)
    cross_re = mult[0] * recorded[0] + mult[1] * recorded[1]
    cross_im = mult[0] * recorded[1] - mult[1] * recorded[0]
    energy = mult[0] * mult[0] + mult[1] * mult[1]
    stacked = jnp.stack([cross_re, cross_im, energy])
    height = stacked.shape[1] // LINE
    breadth = stacked.shape[2] // LINE
    return stacked.reshape(3, height, LINE, breadth, LINE).sum(axis=(2, 4))


def on_device(data, source_term):
    row_count = data.shape[1]
    col_count = data.shape[2]
    recorded = data.astype(jnp.float32)
    weight_re = source_term[0][:, None]
    weight_im = source_term[1][:, None]
    scaled = jnp.stack(
        [
            weight_re * recorded[0] - weight_im * recorded[1],
            weight_re * recorded[1] + weight_im * recorded[0],
        ]
    ).astype(jnp.bfloat16)
    row_panel = lax.all_gather(data, "rcv", axis=2, tiled=True)
    product = complex_product(row_panel, lax.all_gather(scaled, "src", axis=1, tiled=True))
    multiples = product.astype(jnp.bfloat16)
    block_rows = row_count // LINE
    block_cols = col_count // LINE
    local_sums = line_block_sums(multiples, data)
    sums = with_halo(local_sums, (("src", 1), ("rcv", 2)), 1)
    window = jnp.zeros((3, block_rows, block_cols), jnp.float32)
    for shift_row in range(3):
        for shift_col in range(3):
            window = (
                window
                + sums[:, shift_row : shift_row + block_rows, shift_col : shift_col + block_cols]
            )
    filter_re = window[0] / (window[2] + stabiliser)
    filter_im = window[1] / (window[2] + stabiliser)
    mult = multiples.astype(jnp.float32).reshape(2, block_rows, LINE, block_cols, LINE)
    coef_re = filter_re[:, None, :, None]
    coef_im = filter_im[:, None, :, None]
    matched_re = coef_re * mult[0] - coef_im * mult[1]
    matched_im = coef_re * mult[1] + coef_im * mult[0]
    matched = jnp.stack([matched_re, matched_im]).reshape(2, row_count, col_count)
    return matched.astype(jnp.bfloat16)


def solution(mesh):
    in_specs = (P(None, "src", "rcv"), P(None, "src"))
    out_specs = P(None, "src", "rcv")
    return jax.shard_map(
        on_device, mesh=mesh, in_specs=in_specs, out_specs=out_specs, check_vma=False
    )
```

profile of v0, /device:TPU:1, one launch (start us, length us, event | category | flops | bytes accessed | tf_op | source)
XLA Modules:
  0.0 742.9 jit_solution(9772887211352254755)
XLA Ops:
  6.5 0.0 all-gather.5.cloned.1.call-start
  6.5 0.7 all-gather.5.cloned.1.call-update
  7.3 0.0 all-gather.3.cloned.1.call-start
  7.3 6.6 copy.5
  13.9 3.1 convert_element_type.4
  17.0 0.0 copy-done.2
  17.0 0.0 copy-start
  17.1 1.4 subtract_convert_fusion.2
  18.5 3.7 copy-done
  22.1 2.8 pad_maximum_fusion
  25.0 0.0 all-gather.3.cloned.1.call-update
  25.0 308.7 %all-gather.5.cloned.1.call-done = bf16[2,768,6144]{2,1,0:T(8,128)(2,1)} async-done(((bf16[2,768,1536]{2,1,0:T(8,128)(2,1)}), bf16[2,768,6144]{2,1,0:T(8,128)(2,1)}) %all-gather.5.cloned.1.call-update) | async-done | bytes 18874384 | tf_op jit(solution)/shard_map/all_gather | solution.py:59
  333.6 180.0 %all-gather.3.cloned.1.call-done = bf16[2,6144,1536]{1,2,0:T(8,128)(2,1)} async-done(((bf16[2,768,1536]{1,2,0:T(8,128)(2,1)}), bf16[2,6144,1536]{1,2,0:T(8,128)(2,1)}) %all-gather.3.cloned.1.call-update) | async-done | bytes 37748752 | tf_op jit(solution)/shard_map/all_gather | solution.py:60
  513.6 21.9 %fusion = f32[1536,768]{1,0:T(8,128)} fusion(bf16[2,6144,1536]{1,2,0:T(8,128)(2,1)} %all-gather.3.cloned.1.call-done, bf16[2,768,6144]{2,1,0:T(8,128)(2,1)} %all-gather.5.cloned.1.call-done), kind=kOutput, calls=%fused_computation.3 | convolution fusion | flops 14495514624 | bytes 33030144 | tf_op jit(solution)/shard_map/dot_general | solution.py:29
  535.5 21.9 %fusion.1 = f32[1536,768]{1,0:T(8,128)} fusion(bf16[2,6144,1536]{1,2,0:T(8,128)(2,1)} %all-gather.3.cloned.1.call-done, bf16[2,768,6144]{2,1,0:T(8,128)(2,1)} %all-gather.5.cloned.1.call-done), kind=kOutput, calls=%fused_computation.4 | convolution fusion | flops 14495514624 | bytes 33030144 | tf_op jit(solution)/shard_map/dot_general | solution.py:26
  557.3 21.2 %fusion.5 = bf16[1,768,1536]{1,2,0:T(8,128)(2,1)S(1)} fusion(f32[1536,768]{1,0:T(8,128)} %fusion, bf16[2,768,6144]{2,1,0:T(8,128)(2,1)} %all-gather.5.cloned.1.call-done, bf16[2,6144,1536]{1,2,0:T(8,128)(2,1)} %all-gather.3.cloned.1.call-done), kind=kOutput, calls=%fused_computation.22 | convolution fusion | flops 14497873920 | bytes 35389440 | tf_op jit(solution)/shard_map/dot_general | solution.py:29
  578.5 22.1 %fusion.4 = bf16[1,768,1536]{1,2,0:T(8,128)(2,1)} fusion(f32[1536,768]{1,0:T(8,128)} %fusion.1, bf16[2,768,6144]{2,1,0:T(8,128)(2,1)} %all-gather.5.cloned.1.call-done, bf16[2,6144,1536]{1,2,0:T(8,128)(2,1)} %all-gather.3.cloned.1.call-done), kind=kOutput, calls=%fused_computation.21 | convolution fusion | flops 14497873920 | bytes 35389440 | tf_op jit(solution)/shard_map/dot_general | solution.py:26
  600.6 2.3 maximum_convert_fusion
  602.9 0.0 copy-start.1
  602.9 11.5 %multiply_add_fusion.1 = (f32[1,768,1536]{1,2,0:T(8,128)}, f32[1,768,1536]{1,2,0:T(8,128)}, f32[1,768,1536]{1,2,0:T(8,128)}) fusion(f32[2,768,1536]{1,2,0:T(8,128)} %copy-done, f32[2,768,1536]{1,2,0:T(8,128)S(1)} %maximum_convert_fusion), kind=kLoop, calls=%fused_computation.16 | loop fusion | flops 10616832 | bytes 33030144 | tf_op jit(solution)/shard_map/add | solution.py:38
  614.5 0.0 copy-done.1
  614.5 6.0 copy.6
  620.5 7.7 %stack.39 = f32[1,12,64,24,64]{4,3,2,1,0:T(8,128)} reshape(f32[1,768,1536]{2,1,0:T(8,128)} %copy.6) | data formatting | bytes 9437184 | tf_op jit(solution)/shard_map/stack | solution.py:41
  628.2 6.0 copy.7
  634.3 7.7 %stack.40 = f32[1,12,64,24,64]{4,3,2,1,0:T(8,128)} reshape(f32[1,768,1536]{2,1,0:T(8,128)} %copy.7) | data formatting | bytes 9437184 | tf_op jit(solution)/shard_map/stack | solution.py:41
  642.0 6.0 copy.8
  648.0 7.7 %stack.41 = f32[1,12,64,24,64]{4,3,2,1,0:T(8,128)} reshape(f32[1,768,1536]{2,1,0:T(8,128)} %copy.8) | data formatting | bytes 9437184 | tf_op jit(solution)/shard_map/stack | solution.py:41
  655.7 9.8 %maximum_reduce_fusion = f32[3,12,24]{2,1,0:T(8,128)S(1)} fusion(f32[1,12,64,24,64]{4,3,2,1,0:T(8,128)} %stack.41, f32[1,12,64,24,64]{4,3,2,1,0:T(8,128)} %stack.40, f32[1,12,64,24,64]{4,3,2,1,0:T(8,128)} %stack.39), kind=kLoop, calls=%fused_computation | loop fusion | flops 10615968 | bytes 14159232 | tf_op jit(solution)/shard_map/reduce_sum | solution.py:44
  665.5 3.2 collective-permute-start
  668.7 1.9 collective-permute-start.1
  670.7 0.0 collective-permute-done
  670.7 3.0 collective-permute-done.1
  673.7 0.1 fusion.11
  673.7 3.1 collective-permute-start.2
  676.8 1.3 collective-permute-start.3
  678.1 0.0 collective-permute-done.2
  678.1 3.3 collective-permute-done.3
  681.4 0.1 maximum_maximum_fusion
  681.5 0.1 slice_add_fusion
  681.6 4.3 mul.108
  685.9 8.6 %mul.109 = f32[1,768,1536]{2,1,0:T(8,128)} reshape(f32[12,64,24,64]{3,2,1,0:T(8,128)} %mul.108) | data formatting | bytes 9437184 | tf_op jit(solution)/shard_map/mul | solution.py:78
  694.6 6.1 copy.9
  700.7 4.3 mul.111
  705.0 8.6 %mul.112 = f32[1,768,1536]{2,1,0:T(8,128)} reshape(f32[12,64,24,64]{3,2,1,0:T(8,128)} %mul.111) | data formatting | bytes 9437184 | tf_op jit(solution)/shard_map/mul | solution.py:78
  713.6 6.1 copy.10
  719.7 7.2 subtract_convert_fusion
  726.9 2.5 pad_maximum_fusion.1
  729.4 6.6 copy.13
  (5 shorter events, 0.1 us)
Async XLA Ops:
  6.5 327.1 %all-gather.5.cloned.1.call-start = ((), (), s32[]{:S(2)}) async-start(), calls=%async_computation.1 | async-start | bytes 23592960 | tf_op jit(solution)/shard_map/all_gather | solution.py:59
  7.3 506.3 %all-gather.3.cloned.1.call-start = ((), (), s32[]{:S(2)}) async-start(), calls=%async_computation | async-start | bytes 42467328 | tf_op jit(solution)/shard_map/all_gather | solution.py:60
  13.9 3.1 copy-start.2
  17.0 5.1 copy-start
  602.9 11.5 %copy-start.1 = (f32[2,768,1536]{1,2,0:T(8,128)}, f32[2,768,1536]{1,2,0:T(8,128)S(1)}, u32[]{:S(2)}) copy-start(f32[2,768,1536]{1,2,0:T(8,128)S(1)} %maximum_convert_fusion) | copy-start | bytes 28311556
  665.5 5.2 collective-permute-start
  668.7 4.9 collective-permute-start.1
  673.7 4.4 collective-permute-start.2
  676.8 4.6 collective-permute-start.3
Sparse Core Ops, SparseCore 0:
  8.9 324.6 all-gather.4
  335.6 177.9 all-gather.2
where the time goes:
time: 744 us; the launch traced here: 743 us
  waiting for transfers between devices  496 us (67%)
  local copies, waits for them, and re-layouts  96.4 us (13%)
  matrix products  87 us (12%)
  other arithmetic  40.8 us (5%)
  between operations  13.5 us (2%)
  starting transfers between devices  9.59 us (1%)
    all_gather x1, waiting for transfers between devices, on_device(): row_panel = lax.all_gather(data, 'rcv', axis=2, tiled=True)  309 us
    all_gather x1, waiting for transfers between devices, on_device(): lax.all_gather(scaled, 'src', axis=1, tiled=True)  180 us
    mul x6, local copies, waits for them, and re-layouts, on_device(): matched_re = coef_re * mult[0] - coef_im * mult[1]  38.1 us
    another operation x3, local copies, waits for them, and re-layouts, line_block_sums(): stacked = jnp.stack([cross_re, cross_im, energy])  23.1 us
    dot_general x1, matrix products, complex_product(): jnp.dot(left_part[1], right_part[1], preferred_element_type=jnp.float32)  22.1 us
    dot_general x1, matrix products, complex_product(): jnp.dot(left_part[0], right_part[0], preferred_element_type=jnp.float32)  21.9 us
    dot_general x1, matrix products, complex_product(): jnp.dot(left_part[1], right_part[0], preferred_element_type=jnp.float32)  21.9 us
    dot_general x1, matrix products, complex_product(): jnp.dot(left_part[0], right_part[1], preferred_element_type=jnp.float32)  21.2 us
  transfers between devices with their start and end apart: 6, of which 4 were waited for; matrix products, arithmetic and copies ran while one was open for 2% of the time, Pallas kernels for 0%

commit v1 on v0

v1 whole, which is shorter than its diff:
```python
import functools

import jax
import jax.numpy as jnp
from jax import lax
from jax.experimental import pallas as pl
from jax.experimental.pallas import tpu as pltpu
from jax.sharding import PartitionSpec as P

LINE = 64


stabiliser = 1e-05


def with_halo(block, sides, width):
    for axis, dim in sides:
        count = lax.axis_size(axis)
        forward = [(i, i + 1) for i in range(count - 1)]
        backward = [(target, source) for source, target in forward]
        low = lax.ppermute(
            lax.slice_in_dim(block, block.shape[dim] - width, None, axis=dim), axis, forward
        )
        high = lax.ppermute(lax.slice_in_dim(block, 0, width, axis=dim), axis, backward)
        block = jnp.concatenate([low, block, high], axis=dim)
    return block


def largest(size, choices):
    return next(c for c in choices if size % c == 0)


def product_kernel(options, tile_rows, last, block_of, choice_of, *refs):
    count = 1 + max(max(o) for o in options)
    blocks, rest = refs[:count], list(refs[count:])
    right_ref = rest.pop(0)
    if last:
        total_ref, data_ref, out_ref, sums_ref, left, sems = rest
    else:
        out_ref, left, sems = rest
    phase = pl.program_id(1)
    parts, depth = right_ref.shape[0], right_ref.shape[2]

    @pl.when(jnp.logical_and(pl.program_id(0) == 0, phase == 0))
    def _():
        for p, allowed in enumerate(options):
            for c in allowed:
                @pl.when(choice_of[p] == c)
                def _():
                    pltpu.make_async_copy(blocks[c], left.at[p], sems.at[p]).start()

    @pl.when(pl.program_id(0) == 0)
    def _():
        pltpu.make_async_copy(blocks[0], left.at[phase], sems.at[phase]).wait()

    def products(rows):
        real_part = imag_part = None
        for q in range(parts):
            span = slice(q * depth, (q + 1) * depth)
            a_re, a_im = left[phase, 0, rows, span], left[phase, 1, rows, span]
            b_re, b_im = right_ref[q, 0], right_ref[q, 1]
            dot = functools.partial(jnp.dot, preferred_element_type=jnp.float32)
            re = dot(a_re, b_re) - dot(a_im, b_im)
            im = dot(a_re, b_im) + dot(a_im, b_re)
            real_part = re if q == 0 else real_part + re
            imag_part = im if q == 0 else imag_part + im
        return real_part, imag_part

    tiles = left.shape[2] // tile_rows

    @pl.loop(0, tiles)
    def _(tile):
        rows = pl.ds(pl.multiple_of(tile * tile_rows, tile_rows), tile_rows)
        re, im = products(rows)
        if last:
            re = (re + total_ref[0, rows, :]).astype(jnp.bfloat16)
            im = (im + total_ref[1, rows, :]).astype(jnp.bfloat16)
            out_ref[0, rows, :] = re
            out_ref[1, rows, :] = im
            re, im = re.astype(jnp.float32), im.astype(jnp.float32)
            d_re = data_ref[0, rows, :].astype(jnp.float32)
            d_im = data_ref[1, rows, :].astype(jnp.float32)
            terms = (re * d_re + im * d_im, re * d_im - im * d_re, re * re + im * im)
            for t, term in enumerate(terms):
                folded = term.reshape(tile_rows // LINE, LINE, term.shape[1])
                sums_ref[tile, t] = folded.sum(axis=1)
        else:
            @pl.when(phase == 0)
            def _():
                out_ref[0, rows, :] = re
                out_ref[1, rows, :] = im

            @pl.when(phase > 0)
            def _():
                out_ref[0, rows, :] += re
                out_ref[1, rows, :] += im


def multiply(blocks, options, block_of, choice_of, panel, total=None, data=None):
    last = total is not None
    _, rows, width = blocks[0].shape
    depth, columns = panel.shape[2], panel.shape[3]
    parts = width // depth
    wide = largest(columns, (512, 384, 256, 128))
    tile_rows = largest(rows, (256, 128, 64))
    tiles = rows // tile_rows
    phases = len(options)

    def column(j, p, *_):
        return (0, 0, j)

    whole = pl.BlockSpec((2, rows, wide), column)
    in_specs = [pl.BlockSpec(memory_space=pl.ANY)] * len(blocks) + [
        pl.BlockSpec((parts, 2, depth, wide), lambda j, p, b, c: (b[p], 0, 0, j))
    ]
    operands = list(blocks) + [panel]
    if last:
        in_specs += [whole, whole]
        operands += [total, data]
        lines = tile_rows // LINE
        out_shape = (
            jax.ShapeDtypeStruct((2, rows, columns), jnp.bfloat16),
            jax.ShapeDtypeStruct((tiles, 3, lines, columns), jnp.float32),
        )
        out_specs = (
            whole,
            pl.BlockSpec((tiles, 3, lines, wide), lambda j, p, *_: (0, 0, 0, j)),
        )
    else:
        out_shape = jax.ShapeDtypeStruct((2, rows, columns), jnp.float32)
        out_specs = whole
    return pl.pallas_call(
        functools.partial(product_kernel, options, tile_rows, last),
        out_shape=out_shape,
        grid_spec=pltpu.PrefetchScalarGridSpec(
            num_scalar_prefetch=2,
            grid=(columns // wide, phases),
            in_specs=in_specs,
            out_specs=out_specs,
            scratch_shapes=[
                pltpu.VMEM((phases, 2, rows, width), jnp.bfloat16),
                pltpu.SemaphoreType.DMA((phases,)),
            ],
        ),
        compiler_params=pltpu.CompilerParams(vmem_limit_bytes=48 << 20),
        cost_estimate=pl.CostEstimate(
            flops=8 * rows * width * columns * phases,
            bytes_accessed=4 * phases * rows * width + 4 * phases * width * columns,
            transcendentals=0,
        ),
    )(block_of, choice_of, *operands)


def on_device(data, source_term):
    _, row_count, col_count = data.shape
    count = lax.axis_size("rcv")
    place = lax.axis_index("rcv")
    recorded = data.astype(jnp.float32)
    weight_re = source_term[0][:, None]
    weight_im = source_term[1][:, None]
    scaled = jnp.stack(
        [
            weight_re * recorded[0] - weight_im * recorded[1],
            weight_re * recorded[1] + weight_im * recorded[0],
        ]
    ).astype(jnp.bfloat16)
    panel = lax.all_gather(scaled, "src", axis=0)

    upward = [(i, i + 1) for i in range(count - 1)]
    downward = [(i + 1, i) for i in range(count - 1)]
    ups, downs = [data], [data]
    for _ in range(count - 1):
        ups.append(lax.ppermute(ups[-1], "rcv", upward))
        downs.append(lax.ppermute(downs[-1], "rcv", downward))

    def block_at(step):
        return jnp.where(step <= place, place - step, step)

    inner = count - 2
    blocks = [data] + ups[1 : inner + 1] + downs[1 : inner + 1]
    options = [(0,)] + [
        (step,) + tuple(inner + m for m in range(1, step + 1)) for step in range(1, inner + 1)
    ]
    block_of = jnp.stack([block_at(step) for step in range(inner + 1)]).astype(jnp.int32)
    choice_of = jnp.stack(
        [jnp.where(step <= place, step, inner + step - place) for step in range(inner + 1)]
    ).astype(jnp.int32)
    total = multiply(blocks, options, block_of, choice_of, panel)
    end = count - 1
    multiples, row_sums = multiply(
        [ups[end]] + downs[1:],
        [tuple(range(count))],
        block_at(end).reshape(1).astype(jnp.int32),
        jnp.where(end <= place, 0, end - place).reshape(1).astype(jnp.int32),
        panel,
        total,
        data,
    )

    block_rows = row_count // LINE
    block_cols = col_count // LINE
    local_sums = row_sums.transpose(1, 0, 2, 3).reshape(3, block_rows, block_cols, LINE).sum(axis=3)
    sums = with_halo(local_sums, (("src", 1), ("rcv", 2)), 1)
    window = jnp.zeros((3, block_rows, block_cols), jnp.float32)
    for shift_row in range(3):
        for shift_col in range(3):
            window = (
                window
                + sums[:, shift_row : shift_row + block_rows, shift_col : shift_col + block_cols]
            )
    coef = jnp.repeat(window[:2] / (window[2:] + stabiliser), LINE, axis=2)
    mult = multiples.reshape(2, block_rows, LINE, col_count).astype(jnp.float32)
    coef_re = coef[0][:, None, :]
    coef_im = coef[1][:, None, :]
    matched = jnp.stack(
        [coef_re * mult[0] - coef_im * mult[1], coef_re * mult[1] + coef_im * mult[0]]
    )
    return matched.astype(jnp.bfloat16).reshape(2, row_count, col_count)


def solution(mesh):
    in_specs = (P(None, "src", "rcv"), P(None, "src"))
    out_specs = P(None, "src", "rcv")
    return jax.shard_map(
        on_device, mesh=mesh, in_specs=in_specs, out_specs=out_specs, check_vma=False
    )
```

time: 744 us -> 404 us (0.54)
  waiting for transfers between devices: 496 us -> 238 us
  matrix products: 87 us -> 0 us
  Pallas kernels: 0 us -> 82.4 us
  local copies, waits for them, and re-layouts: 96.4 us -> 15.5 us
  starting transfers between devices: 9.59 us -> 34.2 us
  other arithmetic: 40.8 us -> 17.1 us
    all_gather x2 -> x1, waiting for transfers between devices: 489 us -> 0.01 us  [on_device(): panel = lax.all_gather(scaled, 'src', axis=0)]
    ppermute x0 -> x6, waiting for transfers between devices: none -> 235 us  [the longest x3 234 us: on_device(): downs.append(lax.ppermute(downs[-1], 'rcv', downward))]
    dot_general x4 -> x0, matrix products: 87 us -> none  [the longest x1 22.1 us: complex_product(): jnp.dot(left_part[1], right_part[1], preferred_element_type=jnp.float32)]
    pallas_call x0 -> x2, Pallas kernels: none -> 82.4 us  [multiply(): pl.pallas_call(functools.partial(product_kernel, options, tile_rows, last...]
    mul x6 -> x0, local copies, waits for them, and re-layouts: 38.1 us -> none  [on_device(): matched_re = coef_re * mult[0] - coef_im * mult[1]]
    another operation x4 -> x0, local copies, waits for them, and re-layouts: 29.7 us -> none  [the longest x3 23.1 us: line_block_sums(): stacked = jnp.stack([cross_re, cross_im, energy])]
    ppermute x0 -> x6, starting transfers between devices: none -> 21.1 us  [the longest x3 17.3 us: on_device(): ups.append(lax.ppermute(ups[-1], 'rcv', upward))]
    add x2 -> x0, local copies, waits for them, and re-layouts: 12.1 us -> none  [the longest x1 6.05 us: line_block_sums(): cross_re = mult[0] * recorded[0] + mult[1] * recorded[1]]
  transfers between devices with their start and end apart: 6 -> 11, of which waited for: 4 -> 5; matrix products, arithmetic and copies ran while one was open for 2% -> 2% of each run, Pallas kernels for 0% -> 14%
where the time goes in v1:
time: 404 us; the launch traced here: 401 us
  waiting for transfers between devices  238 us (59%)
  Pallas kernels  82.4 us (20%)
  starting transfers between devices  34.2 us (8%)
  other arithmetic  17.1 us (4%)
  local copies, waits for them, and re-layouts  15.5 us (4%)
  between operations  13.6 us (3%)
    ppermute x3, waiting for transfers between devices, on_device(): downs.append(lax.ppermute(downs[-1], 'rcv', downward))  234 us
    pallas_call x2, Pallas kernels, multiply(): pl.pallas_call(functools.partial(product_kernel, options, tile_rows, last...  82.4 us
    ppermute x3, starting transfers between devices, on_device(): ups.append(lax.ppermute(ups[-1], 'rcv', upward))  17.3 us
    ppermute x2, starting transfers between devices, with_halo(): lax.ppermute(lax.slice_in_dim(block, block.shape[dim] - width, None, axis...  9.87 us
  transfers between devices with their start and end apart: 11, of which 5 were waited for; matrix products, arithmetic and copies ran while one was open for 2% of the time, Pallas kernels for 14%

profile of v1, /device:TPU:1, one launch (start us, length us, event | category | flops | bytes accessed | tf_op | source)
XLA Modules:
  0.0 400.7 jit_solution(6052073174908424569)
XLA Ops:
  6.5 0.0 all-gather.2.cloned.1.call-start
  6.5 0.8 slice_reduce_fusion.1
  7.3 3.6 convert_element_type.17
  11.0 2.5 fusion
  13.5 2.6 pad_maximum_fusion
  16.0 0.0 all-gather.2.cloned.1.call-update
  16.0 1.3 collective-permute-start.3
  17.3 5.0 %collective-permute-start = (bf16[2,768,1536]{2,1,0:T(8,128)(2,1)}, bf16[2,768,1536]{2,1,0:T(8,128)(2,1)S(1)}, u32[]{:S(2)}, u32[]{:S(2)}) collective-permute-start(bf16[2,768,1536]{2,1,0:T(8,128)(2,1)} %refs_6_.1), channel_id=1, source_target_pairs={{0,1},{1,2},{2,3},{4,5},{5,6},{6,7},{8,9},{9,10},{10,11},{12,13},{... | collective-permute-start | bytes 14155784 | tf_op jit(solution)/shard_map/ppermute | solution.py:173
  22.3 99.6 %collective-permute-done.3.refs_3_.refs_1_ = bf16[2,768,1536]{2,1,0:T(8,128)(2,1)S(1)} collective-permute-done((bf16[2,768,1536]{2,1,0:T(8,128)(2,1)}, bf16[2,768,1536]{2,1,0:T(8,128)(2,1)S(1)}, u32[]{:S(2)}, u32[]{:S(2)}) %collective-permute-start.3) | collective-permute-done | bytes 4718624 | tf_op jit(solution)/shard_map/ppermute | solution.py:174
  121.9 0.0 copy-start.2
  121.9 2.2 copy-done.2
  124.1 1.3 collective-permute-start.4
  125.4 0.0 collective-permute-done.refs_1_
  125.4 0.0 copy-start.3
  125.4 6.2 %collective-permute-start.1 = (bf16[2,768,1536]{2,1,0:T(8,128)(2,1)S(1)}, bf16[2,768,1536]{2,1,0:T(8,128)(2,1)}, u32[]{:S(2)}, u32[]{:S(2)}) collective-permute-start(bf16[2,768,1536]{2,1,0:T(8,128)(2,1)S(1)} %collective-permute-done.refs_1_), channel_id=1, source_target_pairs={{0,1},{1,2},{2,3},{4,5},{5,6},{6,7},{8,9},{9,10},{10,11},{12,13},{... | collective-permute-start | bytes 14155784 | tf_op jit(solution)/shard_map/ppermute | solution.py:173
  131.6 96.7 %collective-permute-done.4.refs_4_.refs_2_ = bf16[2,768,1536]{2,1,0:T(8,128)(2,1)} collective-permute-done((bf16[2,768,1536]{2,1,0:T(8,128)(2,1)S(1)}, bf16[2,768,1536]{2,1,0:T(8,128)(2,1)}, u32[]{:S(2)}, u32[]{:S(2)}) %collective-permute-start.4) | collective-permute-done | bytes 4718624 | tf_op jit(solution)/shard_map/ppermute | solution.py:174
  228.3 0.0 copy-done.3
  228.3 1.3 collective-permute-start.5
  229.6 0.0 collective-permute-done.1.refs_2_
  229.6 6.1 %collective-permute-start.2 = (bf16[2,768,1536]{2,1,0:T(8,128)(2,1)}, bf16[2,768,1536]{2,1,0:T(8,128)(2,1)}, u32[]{:S(2)}, u32[]{:S(2)}) collective-permute-start(bf16[2,768,1536]{2,1,0:T(8,128)(2,1)} %collective-permute-done.1.refs_2_), channel_id=1, source_target_pairs={{0,1},{1,2},{2,3},{4,5},{5,6},{6,7},{8,9},{9,10},{10,11},{12,13},{... | collective-permute-start | bytes 14155784 | tf_op jit(solution)/shard_map/ppermute | solution.py:173
  235.7 0.1 pad_add_fusion
  235.8 2.3 copy-done
  238.1 55.9 %shard_map.28.refs_5_ = f32[2,768,1536]{2,1,0:T(8,128)} custom-call(s32[3]{0:T(128)S(1)} %get-tuple-element.25.block_of, s32[3]{0:T(128)S(1)} %get-tuple-element.26.choice_of, bf16[2,768,1536]{2,1,0:T(8,128)(2,1)S(1)} %copy-done, bf16[2,768,1536]{2,1,0:T(8,128)(2,1)} %copy-done.3, bf16[2,768,1536]{2,1,0:T(8,128)(2,1)} %collective-permute-done.1.refs_2_, ...), custom_call_target="tpu_custom_call" | custom-call | flops 43486543872 | bytes 42467328 | tf_op jit(solution)/shard_map/pallas_call | solution.py:132
  294.0 37.7 %collective-permute-done.5.refs_3_ = bf16[2,768,1536]{2,1,0:T(8,128)(2,1)} collective-permute-done((bf16[2,768,1536]{2,1,0:T(8,128)(2,1)}, bf16[2,768,1536]{2,1,0:T(8,128)(2,1)}, u32[]{:S(2)}, u32[]{:S(2)}) %collective-permute-start.5) | collective-permute-done | bytes 4718624 | tf_op jit(solution)/shard_map/ppermute | solution.py:174
  331.7 0.9 collective-permute-done.2.refs_0_
  332.6 26.5 %shard_map.29 = (bf16[2,768,1536]{2,1,0:T(8,128)(2,1)S(1)}, f32[3,3,4,1536]{3,2,1,0:T(4,128)S(1)}) custom-call(s32[1]{0:T(128)} %bitcast.block_of, s32[1]{0:T(128)} %bitcast.1.choice_of, bf16[2,768,1536]{2,1,0:T(8,128)(2,1)} %collective-permute-done.2.refs_0_, bf16[2,768,1536]{2,1,0:T(8,128)(2,1)} %copy-done.2, ...), custom_call_target="tpu_custom_call" | custom-call | flops 14495514624 | bytes 14155776 | tf_op jit(solution)/shard_map/pallas_call | solution.py:132
  359.1 0.0 copy-start.1
  359.2 2.2 copy-done.1
  361.4 0.2 reshape.88
  361.5 0.2 reduce_sum.9
  361.8 5.8 %collective-permute-start.6 = (f32[3,1,24]{2,1,0:T(1,128)S(1)}, f32[3,1,24]{2,1,0:T(1,128)S(1)}, u32[]{:S(2)}, u32[]{:S(2)}) collective-permute-start(f32[3,1,24]{2,1,0:T(1,128)S(1)} %get-tuple-element.21), channel_id=1, source_target_pairs={{0,4},{4,8},{8,12},{12,16},{16,20},{20,24},{24,28},{1,5},{5,9},{9,... | collective-permute-start | bytes 872 | tf_op jit(solution)/shard_map/ppermute | solution.py:21
  367.5 1.9 collective-permute-start.7
  369.5 0.0 collective-permute-done.6
  369.5 3.0 collective-permute-done.7
  372.4 0.1 fusion.7
  372.5 4.1 %collective-permute-start.8 = (f32[3,14,1]{2,1,0:T(8,128)S(1)}, f32[3,14,1]{2,1,0:T(8,128)S(1)}, u32[]{:S(2)}, u32[]{:S(2)}) collective-permute-start(f32[3,14,1]{2,1,0:T(8,128)S(1)} %get-tuple-element.19), channel_id=1, source_target_pairs={{0,1},{1,2},{2,3},{4,5},{5,6},{6,7},{8,9},{9,10},{10,11},{12,13},{... | collective-permute-start | bytes 512 | tf_op jit(solution)/shard_map/ppermute | solution.py:21
  376.6 1.3 collective-permute-start.9
  377.9 7.4 %fusion.6 = (f32[1,768,1536]{2,1,0:T(8,128)}, f32[1,768,1536]{2,1,0:T(8,128)}) fusion(bf16[2,768,1536]{2,1,0:T(8,128)(2,1)} %copy-done.1), kind=kLoop, calls=%fused_computation.30 | loop fusion | bytes 18874368 | tf_op jit(solution)/shard_map/slice | solution.py:216
  385.3 0.0 collective-permute-done.8
  385.3 0.0 collective-permute-done.9
  385.3 0.1 maximum_maximum_fusion
  385.4 0.1 slice_add_fusion
  385.5 0.1 broadcast_in_dim.9
  385.6 0.1 broadcast_in_dim.10
  385.7 0.1 broadcast_in_dim.11
  385.8 0.1 broadcast_in_dim.12
  385.9 5.4 %subtract_convert_fusion = (bf16[1,12,64,1536]{3,2,1,0:T(8,128)(2,1)S(1)}, bf16[1,12,64,1536]{3,2,1,0:T(8,128)(2,1)S(1)}) fusion(f32[1,12,64,1536]{3,2,1,0:T(8,128)} %bitcast.24, f32[1,12,64,1536]{3,2,1,0:T(8,128)} %bitcast.25, f32[12,1536]{1,0:T(8,128)S(1)} %broadcast_in_dim.12, f32[12,1536]{1,0:T(8,128)S(1)} %broadcast_in_dim.10), kind=kLoop, calls=%fused_computation.3 | loop fusion | flops 9437184 | bytes 14303232 | tf_op jit(solution)/shard_map/convert.3
  391.3 2.6 pad_maximum_fusion.1
  (8 shorter events, 0.1 us)
Async XLA Ops:
  6.5 229.2 %all-gather.2.cloned.1.call-start = ((), (), s32[]{:S(2)}) async-start(), calls=%async_computation | async-start | bytes 42467328 | tf_op jit(solution)/shard_map/all_gather | solution.py:167
  16.0 105.9 %collective-permute-start.3 = (bf16[2,768,1536]{2,1,0:T(8,128)(2,1)}, bf16[2,768,1536]{2,1,0:T(8,128)(2,1)S(1)}, u32[]{:S(2)}, u32[]{:S(2)}) collective-permute-start(bf16[2,768,1536]{2,1,0:T(8,128)(2,1)} %refs_6_.1), channel_id=1, source_target_pairs={{1,0},{2,1},{3,2},{5,4},{6,5},{7,6},{9,8},{10,9},{11,10},{13,12},{... | collective-permute-start | bytes 14155784 | tf_op jit(solution)/shard_map/ppermute | solution.py:174
  17.3 108.1 %collective-permute-start = (bf16[2,768,1536]{2,1,0:T(8,128)(2,1)}, bf16[2,768,1536]{2,1,0:T(8,128)(2,1)S(1)}, u32[]{:S(2)}, u32[]{:S(2)}) collective-permute-start(bf16[2,768,1536]{2,1,0:T(8,128)(2,1)} %refs_6_.1), channel_id=1, source_target_pairs={{0,1},{1,2},{2,3},{4,5},{5,6},{6,7},{8,9},{9,10},{10,11},{12,13},{... | collective-permute-start | bytes 14155784 | tf_op jit(solution)/shard_map/ppermute | solution.py:173
  121.9 2.2 copy-start.2
  124.1 104.2 %collective-permute-start.4 = (bf16[2,768,1536]{2,1,0:T(8,128)(2,1)S(1)}, bf16[2,768,1536]{2,1,0:T(8,128)(2,1)}, u32[]{:S(2)}, u32[]{:S(2)}) collective-permute-start(bf16[2,768,1536]{2,1,0:T(8,128)(2,1)S(1)} %collective-permute-done.3.refs_3_.refs_1_), channel_id=1, source_target_pairs={{1,0},{2,1},{3,2},{5,4},{6,5},{7,6},{9,8},{10,9},{11,10},{13,12},{... | collective-permute-start | bytes 14155784 | tf_op jit(solution)/shard_map/ppermute | solution.py:174
  125.4 102.9 %copy-start.3 = (bf16[2,768,1536]{2,1,0:T(8,128)(2,1)}, bf16[2,768,1536]{2,1,0:T(8,128)(2,1)S(1)}, u32[]{:S(2)}) copy-start(bf16[2,768,1536]{2,1,0:T(8,128)(2,1)S(1)} %collective-permute-done.refs_1_) | copy-start | bytes 14155780
  125.4 104.2 %collective-permute-start.1 = (bf16[2,768,1536]{2,1,0:T(8,128)(2,1)S(1)}, bf16[2,768,1536]{2,1,0:T(8,128)(2,1)}, u32[]{:S(2)}, u32[]{:S(2)}) collective-permute-start(bf16[2,768,1536]{2,1,0:T(8,128)(2,1)S(1)} %collective-permute-done.refs_1_), channel_id=1, source_target_pairs={{0,1},{1,2},{2,3},{4,5},{5,6},{6,7},{8,9},{9,10},{10,11},{12,13},{... | collective-permute-start | bytes 14155784 | tf_op jit(solution)/shard_map/ppermute | solution.py:173
  228.3 103.5 %collective-permute-start.5 = (bf16[2,768,1536]{2,1,0:T(8,128)(2,1)}, bf16[2,768,1536]{2,1,0:T(8,128)(2,1)}, u32[]{:S(2)}, u32[]{:S(2)}) collective-permute-start(bf16[2,768,1536]{2,1,0:T(8,128)(2,1)} %collective-permute-done.4.refs_4_.refs_2_), channel_id=1, source_target_pairs={{1,0},{2,1},{3,2},{5,4},{6,5},{7,6},{9,8},{10,9},{11,10},{13,12},{... | collective-permute-start | bytes 14155784 | tf_op jit(solution)/shard_map/ppermute | solution.py:174
  229.6 103.1 %collective-permute-start.2 = (bf16[2,768,1536]{2,1,0:T(8,128)(2,1)}, bf16[2,768,1536]{2,1,0:T(8,128)(2,1)}, u32[]{:S(2)}, u32[]{:S(2)}) collective-permute-start(bf16[2,768,1536]{2,1,0:T(8,128)(2,1)} %collective-permute-done.1.refs_2_), channel_id=1, source_target_pairs={{0,1},{1,2},{2,3},{4,5},{5,6},{6,7},{8,9},{9,10},{10,11},{12,13},{... | collective-permute-start | bytes 14155784 | tf_op jit(solution)/shard_map/ppermute | solution.py:173
  235.8 2.3 copy-start
  359.1 2.2 copy-start.1
  361.8 7.7 %collective-permute-start.6 = (f32[3,1,24]{2,1,0:T(1,128)S(1)}, f32[3,1,24]{2,1,0:T(1,128)S(1)}, u32[]{:S(2)}, u32[]{:S(2)}) collective-permute-start(f32[3,1,24]{2,1,0:T(1,128)S(1)} %get-tuple-element.21), channel_id=1, source_target_pairs={{0,4},{4,8},{8,12},{12,16},{16,20},{20,24},{24,28},{1,5},{5,9},{9,... | collective-permute-start | bytes 872 | tf_op jit(solution)/shard_map/ppermute | solution.py:21
  367.5 4.9 %collective-permute-start.7 = (f32[3,1,24]{2,1,0:T(1,128)S(1)}, f32[3,1,24]{2,1,0:T(1,128)S(1)}, u32[]{:S(2)}, u32[]{:S(2)}) collective-permute-start(f32[3,1,24]{2,1,0:T(1,128)S(1)} %get-tuple-element.22), channel_id=1, source_target_pairs={{4,0},{8,4},{12,8},{16,12},{20,16},{24,20},{28,24},{5,1},{9,5},{13... | collective-permute-start | bytes 872 | tf_op jit(solution)/shard_map/ppermute | solution.py:24
  372.5 12.8 %collective-permute-start.8 = (f32[3,14,1]{2,1,0:T(8,128)S(1)}, f32[3,14,1]{2,1,0:T(8,128)S(1)}, u32[]{:S(2)}, u32[]{:S(2)}) collective-permute-start(f32[3,14,1]{2,1,0:T(8,128)S(1)} %get-tuple-element.19), channel_id=1, source_target_pairs={{0,1},{1,2},{2,3},{4,5},{5,6},{6,7},{8,9},{9,10},{10,11},{12,13},{... | collective-permute-start | bytes 512 | tf_op jit(solution)/shard_map/ppermute | solution.py:21
  376.6 8.7 %collective-permute-start.9 = (f32[3,14,1]{2,1,0:T(8,128)S(1)}, f32[3,14,1]{2,1,0:T(8,128)S(1)}, u32[]{:S(2)}, u32[]{:S(2)}) collective-permute-start(f32[3,14,1]{2,1,0:T(8,128)S(1)} %get-tuple-element.20), channel_id=1, source_target_pairs={{1,0},{2,1},{3,2},{5,4},{6,5},{7,6},{9,8},{10,9},{11,10},{13,12},{... | collective-permute-start | bytes 512 | tf_op jit(solution)/shard_map/ppermute | solution.py:24
Sparse Core Ops, SparseCore 0:
  16.2 182.0 all-gather.1

commit v2 on v1

--- a/solution.py
+++ b/solution.py
@@ -30,16 +30,25 @@
     return next(c for c in choices if size % c == 0)
 
 
-def product_kernel(options, tile_rows, last, block_of, choice_of, *refs):
-    count = 1 + max(max(o) for o in options)
+def product_kernel(options, tile_rows, last, handed, pieces, block_of, choice_of, *refs):
+    count = pieces * (1 + max(max(o) for o in options))
     blocks, rest = refs[:count], list(refs[count:])
     right_ref = rest.pop(0)
     if last:
-        total_ref, data_ref, out_ref, sums_ref, left, sems = rest
+        total_ref, data_ref = rest.pop(0), rest.pop(0)
+        if handed:
+            rest.pop(0)
+        out_ref, sums_ref, left, sems = rest
     else:
         out_ref, left, sems = rest
     phase = pl.program_id(1)
     parts, depth = right_ref.shape[0], right_ref.shape[2]
+
+    def load(c, p, piece):
+        start = sum(blocks[i].shape[1] for i in range(piece))
+        source = blocks[c * pieces + piece]
+        rows = pl.ds(start, source.shape[1])
+        return pltpu.make_async_copy(source, left.at[p, :, rows], sems.at[p, piece])
 
     @pl.when(jnp.logical_and(pl.program_id(0) == 0, phase == 0))
     def _():
@@ -47,11 +56,13 @@
             for c in allowed:
                 @pl.when(choice_of[p] == c)
                 def _():
-                    pltpu.make_async_copy(blocks[c], left.at[p], sems.at[p]).start()
+                    for piece in range(pieces):
+                        load(c, p, piece).start()
 
     @pl.when(pl.program_id(0) == 0)
     def _():
-        pltpu.make_async_copy(blocks[0], left.at[phase], sems.at[phase]).wait()
+        for piece in range(pieces):
+            load(0, phase, piece).wait()
 
     def products(rows):
         real_part = imag_part = None
@@ -96,30 +107,37 @@
                 out_ref[1, rows, :] += im
 
 
-def multiply(blocks, options, block_of, choice_of, panel, total=None, data=None):
-    last = total is not None
-    _, rows, width = blocks[0].shape
+def multiply(blocks, options, block_of, choice_of, panel, first_row=0, last=None):
+    pieces = len(blocks[0])
+    rows = sum(piece.shape[1] for piece in blocks[0])
+    width = blocks[0][0].shape[2]
     depth, columns = panel.shape[2], panel.shape[3]
     parts = width // depth
     wide = largest(columns, (512, 384, 256, 128))
     tile_rows = largest(rows, (256, 128, 64))
     tiles = rows // tile_rows
     phases = len(options)
-
-    def column(j, p, *_):
-        return (0, 0, j)
-
-    whole = pl.BlockSpec((2, rows, wide), column)
-    in_specs = [pl.BlockSpec(memory_space=pl.ANY)] * len(blocks) + [
+    place = first_row // rows
+
+    whole = pl.BlockSpec((2, rows, wide), lambda j, p, *_: (0, place, j))
+    operands = [piece for block in blocks for piece in block] + [panel]
+    in_specs = [pl.BlockSpec(memory_space=pl.ANY)] * (len(operands) - 1) + [
         pl.BlockSpec((parts, 2, depth, wide), lambda j, p, b, c: (b[p], 0, 0, j))
     ]
-    operands = list(blocks) + [panel]
-    if last:
+    aliases = {}
+    handed = False
+    if last is not None:
+        total, data, out = last
+        operands += [total, data]
         in_specs += [whole, whole]
-        operands += [total, data]
+        if out is not None:
+            handed = True
+            aliases = {2 + len(operands): 0}
+            operands.append(out)
+            in_specs.append(pl.BlockSpec(memory_space=pl.ANY))
         lines = tile_rows // LINE
         out_shape = (
-            jax.ShapeDtypeStruct((2, rows, columns), jnp.bfloat16),
+            jax.ShapeDtypeStruct(data.shape, jnp.bfloat16),
             jax.ShapeDtypeStruct((tiles, 3, lines, columns), jnp.float32),
         )
         out_specs = (
@@ -130,7 +148,7 @@
         out_shape = jax.ShapeDtypeStruct((2, rows, columns), jnp.float32)
         out_specs = whole
     return pl.pallas_call(
-        functools.partial(product_kernel, options, tile_rows, last),
+        functools.partial(product_kernel, options, tile_rows, last is not None, handed, pieces),
         out_shape=out_shape,
         grid_spec=pltpu.PrefetchScalarGridSpec(
             num_scalar_prefetch=2,
@@ -139,9 +157,10 @@
             out_specs=out_specs,
             scratch_shapes=[
                 pltpu.VMEM((phases, 2, rows, width), jnp.bfloat16),
-                pltpu.SemaphoreType.DMA((phases,)),
+                pltpu.SemaphoreType.DMA((phases, pieces)),
             ],
         ),
+        input_output_aliases=aliases,
         compiler_params=pltpu.CompilerParams(vmem_limit_bytes=48 << 20),
         cost_estimate=pl.CostEstimate(
             flops=8 * rows * width * columns * phases,
@@ -151,33 +170,84 @@
     )(block_of, choice_of, *operands)
 
 
+def scale_kernel(data_ref, weight_ref, out_ref):
+    d_re = data_ref[0].astype(jnp.float32)
+    d_im = data_ref[1].astype(jnp.float32)
+    w_re, w_im = weight_ref[0], weight_ref[1]
+    out_ref[0] = (w_re * d_re - w_im * d_im).astype(jnp.bfloat16)
+    out_ref[1] = (w_re * d_im + w_im * d_re).astype(jnp.bfloat16)
+
+
+def scale(data, source_term):
+    _, rows, columns = data.shape
+    tile = largest(rows, (256, 128, 64))
+    block = pl.BlockSpec((2, tile, columns), lambda i: (0, i, 0))
+    return pl.pallas_call(
+        scale_kernel,
+        out_shape=jax.ShapeDtypeStruct(data.shape, jnp.bfloat16),
+        grid=(rows // tile,),
+        in_specs=[block, pl.BlockSpec((2, tile, 1), lambda i: (0, i, 0))],
+        out_specs=block,
+        compiler_params=pltpu.CompilerParams(vmem_limit_bytes=24 << 20),
+        cost_estimate=pl.CostEstimate(
+            flops=6 * rows * columns, bytes_accessed=8 * rows * columns, transcendentals=0
+        ),
+    )(data, source_term[:, :, None])
+
+
+def match_kernel(mult_ref, coef_ref, out_ref):
+    _, lines, columns = coef_ref.shape[1:]
+    m_re = mult_ref[0].astype(jnp.float32).reshape(lines, LINE, columns)
+    m_im = mult_ref[1].astype(jnp.float32).reshape(lines, LINE, columns)
+    c_re, c_im = coef_ref[0, 0][:, None, :], coef_ref[0, 1][:, None, :]
+    shape = (lines * LINE, columns)
+    out_ref[0] = (c_re * m_re - c_im * m_im).reshape(shape).astype(jnp.bfloat16)
+    out_ref[1] = (c_re * m_im + c_im * m_re).reshape(shape).astype(jnp.bfloat16)
+
+
+def match(multiples, coef):
+    _, rows, columns = multiples.shape
+    tile = largest(rows, (128, 64))
+    lines = tile // LINE
+    block = pl.BlockSpec((2, tile, columns), lambda i: (0, i, 0))
+    coef = coef.reshape(2, rows // tile, lines, columns).transpose(1, 0, 2, 3)
+    return pl.pallas_call(
+        match_kernel,
+        out_shape=jax.ShapeDtypeStruct(multiples.shape, jnp.bfloat16),
+        grid=(rows // tile,),
+        in_specs=[block, pl.BlockSpec((1, 2, lines, columns), lambda i: (i, 0, 0, 0))],
+        out_specs=block,
+        compiler_params=pltpu.CompilerParams(vmem_limit_bytes=24 << 20),
+        cost_estimate=pl.CostEstimate(
+            flops=6 * rows * columns, bytes_accessed=8 * rows * columns, transcendentals=0
+        ),
+    )(multiples, coef)
+
+
 def on_device(data, source_term):
     _, row_count, col_count = data.shape
     count = lax.axis_size("rcv")
     place = lax.axis_index("rcv")
-    recorded = data.astype(jnp.float32)
-    weight_re = source_term[0][:, None]
-    weight_im = source_term[1][:, None]
-    scaled = jnp.stack(
-        [
-            weight_re * recorded[0] - weight_im * recorded[1],
-            weight_re * recorded[1] + weight_im * recorded[0],
-        ]
-    ).astype(jnp.bfloat16)
-    panel = lax.all_gather(scaled, "src", axis=0)
-
+    panel = lax.all_gather(scale(data, source_term), "src", axis=0)
+
+    block_rows = row_count // LINE
+    block_cols = col_count // LINE
+    third = row_count // 3
+    edges = [0, 2 * third, row_count] if block_rows % 3 == 0 else [0, row_count]
+    spans = list(zip(edges[:-1], edges[1:]))
     upward = [(i, i + 1) for i in range(count - 1)]
     downward = [(i + 1, i) for i in range(count - 1)]
-    ups, downs = [data], [data]
+    own = [lax.slice_in_dim(data, low, high, axis=1) for low, high in spans]
+    ups, downs = [own], [own]
     for _ in range(count - 1):
-        ups.append(lax.ppermute(ups[-1], "rcv", upward))
-        downs.append(lax.ppermute(downs[-1], "rcv", downward))
+        ups.append([lax.ppermute(piece, "rcv", upward) for piece in ups[-1]])
+        downs.append([lax.ppermute(piece, "rcv", downward) for piece in downs[-1]])
 
     def block_at(step):
         return jnp.where(step <= place, place - step, step)
 
     inner = count - 2
-    blocks = [data] + ups[1 : inner + 1] + downs[1 : inner + 1]
+    blocks = [own] + ups[1 : inner + 1] + downs[1 : inner + 1]
     options = [(0,)] + [
         (step,) + tuple(inner + m for m in range(1, step + 1)) for step in range(1, inner + 1)
     ]
@@ -187,20 +257,21 @@
     ).astype(jnp.int32)
     total = multiply(blocks, options, block_of, choice_of, panel)
     end = count - 1
-    multiples, row_sums = multiply(
-        [ups[end]] + downs[1:],
-        [tuple(range(count))],
-        block_at(end).reshape(1).astype(jnp.int32),
-        jnp.where(end <= place, 0, end - place).reshape(1).astype(jnp.int32),
-        panel,
-        total,
-        data,
-    )
-
-    block_rows = row_count // LINE
-    block_cols = col_count // LINE
-    local_sums = row_sums.transpose(1, 0, 2, 3).reshape(3, block_rows, block_cols, LINE).sum(axis=3)
-    sums = with_halo(local_sums, (("src", 1), ("rcv", 2)), 1)
+    multiples, sums_of = None, []
+    for index in reversed(range(len(spans))):
+        multiples, row_sums = multiply(
+            [[block[index]] for block in [ups[end]] + downs[1:]],
+            [tuple(range(count))],
+            block_at(end).reshape(1).astype(jnp.int32),
+            jnp.where(end <= place, 0, end - place).reshape(1).astype(jnp.int32),
+            panel,
+            spans[index][0],
+            (total, data, multiples),
+        )
+        lines = (spans[index][1] - spans[index][0]) // LINE
+        sums_of.insert(0, row_sums.transpose(1, 0, 2, 3).reshape(3, lines, block_cols, LINE).sum(axis=3))
+
+    sums = with_halo(jnp.concatenate(sums_of, axis=1), (("src", 1), ("rcv", 2)), 1)
     window = jnp.zeros((3, block_rows, block_cols), jnp.float32)
     for shift_row in range(3):
         for shift_col in range(3):
@@ -208,14 +279,7 @@
                 window
                 + sums[:, shift_row : shift_row + block_rows, shift_col : shift_col + block_cols]
             )
-    coef = jnp.repeat(window[:2] / (window[2:] + stabiliser), LINE, axis=2)
-    mult = multiples.reshape(2, block_rows, LINE, col_count).astype(jnp.float32)
-    coef_re = coef[0][:, None, :]
-    coef_im = coef[1][:, None, :]
-    matched = jnp.stack(
-        [coef_re * mult[0] - coef_im * mult[1], coef_re * mult[1] + coef_im * mult[0]]
-    )
-    return matched.astype(jnp.bfloat16).reshape(2, row_count, col_count)
+    return match(multiples, jnp.repeat(window[:2] / (window[2:] + stabiliser), LINE, axis=2))
 
 
 def solution(mesh):

time: 404 us -> 383 us (0.948)
  waiting for transfers between devices: 238 us -> 201 us
  starting transfers between devices: 34.2 us -> 51.3 us
  other arithmetic: 17.1 us -> 0.55 us
  Pallas kernels: 82.4 us -> 96.2 us
    ppermute x6 -> x12, waiting for transfers between devices: 235 us -> 196 us  [the longest x6 195 us: on_device(): downs.append([lax.ppermute(piece, 'rcv', downward) for piece in downs[-1]])]
    ppermute x6 -> x12, starting transfers between devices: 21.1 us -> 38.9 us  [the longest x6 31.2 us: on_device(): ups.append([lax.ppermute(piece, 'rcv', upward) for piece in ups[-1]])]
    another operation x4 -> x0, other arithmetic: 13 us -> none
    pallas_call x2 -> x3, Pallas kernels: 82.4 us -> 89.3 us  [multiply(): pl.pallas_call(functools.partial(product_kernel, options, tile_rows, last...]
    pallas_call x0 -> x2, Pallas kernels: none -> 6.87 us  [the longest x1 4.06 us: match(): pl.pallas_call(match_kernel, out_shape=jax.ShapeDtypeStruct(multiples.sha...]
    unnamed x8 -> x20, local copies, waits for them, and re-layouts: 6.71 us -> 12 us
    slice x3, local copies, waits for them, and re-layouts: 8.16 us -> 4.03 us  [the longest x2 4.02 us: on_device(): own = [lax.slice_in_dim(data, low, high, axis=1) for low, high in spans]]
  transfers between devices with their start and end apart: 11 -> 17, of which waited for: 5 -> 7; matrix products, arithmetic and copies ran while one was open for 2% -> 1% of each run, Pallas kernels for 14% -> 18%
where the time goes in v2:
time: 383 us; the launch traced here: 380 us
  waiting for transfers between devices  201 us (52%)
  Pallas kernels  96.2 us (25%)
  starting transfers between devices  51.3 us (13%)
  local copies, waits for them, and re-layouts  17.6 us (5%)
  between operations  13.8 us (4%)
    ppermute x6, waiting for transfers between devices, on_device(): downs.append([lax.ppermute(piece, 'rcv', downward) for piece in downs[-1]])  195 us
    pallas_call x3, Pallas kernels, multiply(): pl.pallas_call(functools.partial(product_kernel, options, tile_rows, last...  89.3 us
    ppermute x6, starting transfers between devices, on_device(): ups.append([lax.ppermute(piece, 'rcv', upward) for piece in ups[-1]])  31.2 us
    unnamed x20, local copies, waits for them, and re-layouts  12 us
    ppermute x6, starting transfers between devices, on_device(): downs.append([lax.ppermute(piece, 'rcv', downward) for piece in downs[-1]])  7.71 us
  transfers between devices with their start and end apart: 17, of which 7 were waited for; matrix products, arithmetic and copies ran while one was open for 1% of the time, Pallas kernels for 18%

profile of v2, /device:TPU:1, one launch (start us, length us, event | category | flops | bytes accessed | tf_op | source)
XLA Modules:
  0.0 380.3 jit_solution(16486613662800594420)
XLA Ops:
  6.5 1.0 copy.7.weight_ref
  7.5 2.3 copy-done
  9.9 2.8 shard_map.28
  12.7 2.2 copy-done.2
  14.9 2.1 slice.56.refs_0_
  17.0 1.3 collective-permute-start.3
  18.3 6.5 %collective-permute-start = (bf16[2,512,1536]{2,1,0:T(8,128)(2,1)S(1)}, bf16[2,512,1536]{2,1,0:T(8,128)(2,1)}, u32[]{:S(2)}, u32[]{:S(2)}) collective-permute-start(bf16[2,512,1536]{2,1,0:T(8,128)(2,1)S(1)} %slice.56.refs_0_), channel_id=1, source_target_pairs={{0,1},{1,2},{2,3},{4,5},{5,6},{6,7},{8,9},{9,10},{10,11},{12,13},{... | collective-permute-start | bytes 9437192 | tf_op jit(solution)/shard_map/ppermute | solution.py:243
  24.8 1.9 slice.57.refs_1_
  26.7 1.3 collective-permute-start.8
  28.0 4.1 %collective-permute-start.6 = (bf16[2,256,1536]{2,1,0:T(8,128)(2,1)S(1)}, bf16[2,256,1536]{2,1,0:T(8,128)(2,1)S(1)}, u32[]{:S(2)}, u32[]{:S(2)}) collective-permute-start(bf16[2,256,1536]{2,1,0:T(8,128)(2,1)S(1)} %slice.57.refs_1_), channel_id=1, source_target_pairs={{0,1},{1,2},{2,3},{4,5},{5,6},{6,7},{8,9},{9,10},{10,11},{12,13},{... | collective-permute-start | bytes 4718600 | tf_op jit(solution)/shard_map/ppermute | solution.py:243
  32.1 1.1 copy-done.3
  33.3 55.7 %collective-permute-done.3.refs_6_.refs_1_ = bf16[2,512,1536]{2,1,0:T(8,128)(2,1)} collective-permute-done((bf16[2,512,1536]{2,1,0:T(8,128)(2,1)S(1)}, bf16[2,512,1536]{2,1,0:T(8,128)(2,1)}, u32[]{:S(2)}, u32[]{:S(2)}) %collective-permute-start.3) | collective-permute-done | bytes 3145760 | tf_op jit(solution)/shard_map/ppermute | solution.py:244
  89.0 1.3 collective-permute-start.4
  90.3 6.1 %collective-permute-start.1 = (bf16[2,512,1536]{2,1,0:T(8,128)(2,1)}, bf16[2,512,1536]{2,1,0:T(8,128)(2,1)}, u32[]{:S(2)}, u32[]{:S(2)}) collective-permute-start(bf16[2,512,1536]{2,1,0:T(8,128)(2,1)} %collective-permute-done.refs_2_), channel_id=1, source_target_pairs={{0,1},{1,2},{2,3},{4,5},{5,6},{6,7},{8,9},{9,10},{10,11},{12,13},{... | collective-permute-start | bytes 9437192 | tf_op jit(solution)/shard_map/ppermute | solution.py:243
  96.3 26.3 %collective-permute-done.8.refs_7_.refs_1_ = bf16[2,256,1536]{2,1,0:T(8,128)(2,1)S(1)} collective-permute-done((bf16[2,256,1536]{2,1,0:T(8,128)(2,1)S(1)}, bf16[2,256,1536]{2,1,0:T(8,128)(2,1)S(1)}, u32[]{:S(2)}, u32[]{:S(2)}) %collective-permute-start.8) | collective-permute-done | bytes 1572896 | tf_op jit(solution)/shard_map/ppermute | solution.py:244
  122.7 1.3 collective-permute-start.9
  124.0 5.2 %collective-permute-start.7 = (bf16[2,256,1536]{2,1,0:T(8,128)(2,1)S(1)}, bf16[2,256,1536]{2,1,0:T(8,128)(2,1)}, u32[]{:S(2)}, u32[]{:S(2)}) collective-permute-start(bf16[2,256,1536]{2,1,0:T(8,128)(2,1)S(1)} %collective-permute-done.6.refs_3_), channel_id=1, source_target_pairs={{0,1},{1,2},{2,3},{4,5},{5,6},{6,7},{8,9},{9,10},{10,11},{12,13},{... | collective-permute-start | bytes 4718600 | tf_op jit(solution)/shard_map/ppermute | solution.py:243
  129.1 1.1 copy-done.7
  130.3 0.1 pad_add_fusion
  130.4 93.4 %collective-permute-done.9.refs_9_.refs_2_ = bf16[2,256,1536]{2,1,0:T(8,128)(2,1)} collective-permute-done((bf16[2,256,1536]{2,1,0:T(8,128)(2,1)S(1)}, bf16[2,256,1536]{2,1,0:T(8,128)(2,1)}, u32[]{:S(2)}, u32[]{:S(2)}) %collective-permute-start.9) | collective-permute-done | bytes 1572896 | tf_op jit(solution)/shard_map/ppermute | solution.py:244
  223.8 1.3 collective-permute-start.11
  225.1 5.2 %collective-permute-start.10 = (bf16[2,256,1536]{2,1,0:T(8,128)(2,1)}, bf16[2,256,1536]{2,1,0:T(8,128)(2,1)}, u32[]{:S(2)}, u32[]{:S(2)}) collective-permute-start(bf16[2,256,1536]{2,1,0:T(8,128)(2,1)} %collective-permute-done.7.refs_5_), channel_id=1, source_target_pairs={{0,1},{1,2},{2,3},{4,5},{5,6},{6,7},{8,9},{9,10},{10,11},{12,13},{... | collective-permute-start | bytes 4718600 | tf_op jit(solution)/shard_map/ppermute | solution.py:243
  230.3 1.3 collective-permute-start.5
  231.6 4.2 %collective-permute-start.2 = (bf16[2,512,1536]{2,1,0:T(8,128)(2,1)}, bf16[2,512,1536]{2,1,0:T(8,128)(2,1)S(1)}, u32[]{:S(2)}, u32[]{:S(2)}) collective-permute-start(bf16[2,512,1536]{2,1,0:T(8,128)(2,1)} %collective-permute-done.1.refs_4_), channel_id=1, source_target_pairs={{0,1},{1,2},{2,3},{4,5},{5,6},{6,7},{8,9},{9,10},{10,11},{12,13},{... | collective-permute-start | bytes 9437192 | tf_op jit(solution)/shard_map/ppermute | solution.py:243
  235.8 1.4 copy-done.4
  237.2 1.4 copy-done.8
  238.6 57.8 %shard_map.29.refs_5_ = f32[2,768,1536]{2,1,0:T(8,128)} custom-call(s32[3]{0:T(128)S(1)} %get-tuple-element.17.block_of, s32[3]{0:T(128)S(1)} %get-tuple-element.18.choice_of, bf16[2,512,1536]{2,1,0:T(8,128)(2,1)} %copy-done.9, bf16[2,256,1536]{2,1,0:T(8,128)(2,1)S(1)} %copy-done.4, bf16[2,512,1536]{2,1,0:T(8,128)(2,1)} %collective-permute-done.refs_2_, ...), custom_call_target="tpu_custom_call" | custom-call | flops 43486543872 | bytes 42467328 | tf_op jit(solution)/shard_map/pallas_call | solution.py:150
  296.5 12.0 %shard_map.30 = (bf16[2,768,1536]{2,1,0:T(8,128)(2,1)}, f32[1,3,4,1536]{3,2,1,0:T(4,128)S(1)}) custom-call(s32[1]{0:T(128)} %bitcast.block_of, s32[1]{0:T(128)} %bitcast.1.choice_of, bf16[2,256,1536]{2,1,0:T(8,128)(2,1)} %collective-permute-done.10.refs_0_, bf16[2,256,1536]{2,1,0:T(8,128)(2,1)S(1)} %copy-done.6, ...), custom_call_target="tpu_custom_call" | custom-call | flops 4831838208 | bytes 11010048 | tf_op jit(solution)/shard_map/pallas_call | solution.py:150
  308.5 19.6 %collective-permute-done.5.refs_3_ = bf16[2,512,1536]{2,1,0:T(8,128)(2,1)} collective-permute-done((bf16[2,512,1536]{2,1,0:T(8,128)(2,1)}, bf16[2,512,1536]{2,1,0:T(8,128)(2,1)}, u32[]{:S(2)}, u32[]{:S(2)}) %collective-permute-start.5) | collective-permute-done | bytes 3145760 | tf_op jit(solution)/shard_map/ppermute | solution.py:244
  328.1 0.9 collective-permute-done.2.refs_0_
  329.0 19.5 %shard_map.31 = (bf16[2,768,1536]{2,1,0:T(8,128)(2,1)}, f32[2,3,4,1536]{3,2,1,0:T(4,128)S(1)}) custom-call(s32[1]{0:T(128)} %bitcast.block_of, s32[1]{0:T(128)} %bitcast.1.choice_of, bf16[2,512,1536]{2,1,0:T(8,128)(2,1)S(1)} %collective-permute-done.2.refs_0_, ...), custom_call_target="tpu_custom_call", output_to_operand_aliasing={{0}: (9, {})} | custom-call | flops 9663676416 | bytes 12582912 | tf_op jit(solution)/shard_map/pallas_call | solution.py:150
  348.5 0.1 reshape.13
  348.7 0.1 reduce_sum.19
  348.8 4.3 %collective-permute-start.13 = (f32[3,1,24]{2,1,0:T(1,128)S(1)}, f32[3,1,24]{2,1,0:T(1,128)S(1)}, u32[]{:S(2)}, u32[]{:S(2)}) collective-permute-start(f32[3,1,24]{2,1,0:T(1,128)S(1)} %slice.73), channel_id=1, source_target_pairs={{4,0},{8,4},{12,8},{16,12},{20,16},{24,20},{28,24},{5,1},{9,5},{13... | collective-permute-start | bytes 872 | tf_op jit(solution)/shard_map/ppermute | solution.py:24
  353.2 0.1 reshape_transpose.3
  353.3 0.1 reduce_sum.18
  353.4 2.9 collective-permute-start.12
  356.3 0.7 collective-permute-done.12
  357.0 0.1 fusion.4
  357.1 4.0 %collective-permute-start.14 = (f32[3,14,1]{2,1,0:T(8,128)S(1)}, f32[3,14,1]{2,1,0:T(8,128)S(1)}, u32[]{:S(2)}, u32[]{:S(2)}) collective-permute-start(f32[3,14,1]{2,1,0:T(8,128)S(1)} %get-tuple-element.13), channel_id=1, source_target_pairs={{0,1},{1,2},{2,3},{4,5},{5,6},{6,7},{8,9},{9,10},{10,11},{12,13},{... | collective-permute-start | bytes 512 | tf_op jit(solution)/shard_map/ppermute | solution.py:21
  361.1 1.3 collective-permute-start.15
  362.4 4.1 %collective-permute-done.15 = f32[3,14,1]{2,1,0:T(8,128)S(1)} collective-permute-done((f32[3,14,1]{2,1,0:T(8,128)S(1)}, f32[3,14,1]{2,1,0:T(8,128)S(1)}, u32[]{:S(2)}, u32[]{:S(2)}) %collective-permute-start.15) | collective-permute-done | bytes 200 | tf_op jit(solution)/shard_map/ppermute | solution.py:24
  366.5 0.1 maximum_maximum_fusion
  366.6 0.1 slice_add_fusion
  366.7 0.1 broadcast_in_dim.7
  366.9 0.2 reshape_reshape.3
  367.1 2.3 copy-done.1
  369.4 4.1 %shard_map.32 = bf16[2,768,1536]{2,1,0:T(8,128)(2,1)} custom-call(bf16[2,768,1536]{2,1,0:T(8,128)(2,1)S(1)} %copy-done.1, f32[6,2,2,1536]{3,2,1,0:T(2,128)S(1)} %bitcast.18), custom_call_target="tpu_custom_call" | custom-call | flops 7077888 | bytes 9437184 | tf_op jit(solution)/shard_map/pallas_call | solution.py:214
  (32 shorter events, 0.2 us)
Async XLA Ops:
  6.5 229.3 %all-gather.3.cloned.1.call-start = ((), (), s32[]{:S(2)}) async-start(), calls=%async_computation | async-start | bytes 42467328 | tf_op jit(solution)/shard_map/all_gather | solution.py:231
  7.5 2.3 copy-start
  12.7 2.2 copy-start.2
  17.0 112.1 %copy-start.9 = (bf16[2,512,1536]{2,1,0:T(8,128)(2,1)}, bf16[2,512,1536]{2,1,0:T(8,128)(2,1)S(1)}, u32[]{:S(2)}) copy-start(bf16[2,512,1536]{2,1,0:T(8,128)(2,1)S(1)} %slice.56.refs_0_) | copy-start | bytes 9437188
  17.0 72.0 %collective-permute-start.3 = (bf16[2,512,1536]{2,1,0:T(8,128)(2,1)S(1)}, bf16[2,512,1536]{2,1,0:T(8,128)(2,1)}, u32[]{:S(2)}, u32[]{:S(2)}) collective-permute-start(bf16[2,512,1536]{2,1,0:T(8,128)(2,1)S(1)} %slice.56.refs_0_), channel_id=1, source_target_pairs={{1,0},{2,1},{3,2},{5,4},{6,5},{7,6},{9,8},{10,9},{11,10},{13,12},{... | collective-permute-start | bytes 9437192 | tf_op jit(solution)/shard_map/ppermute | solution.py:244
  18.3 72.0 %collective-permute-start = (bf16[2,512,1536]{2,1,0:T(8,128)(2,1)S(1)}, bf16[2,512,1536]{2,1,0:T(8,128)(2,1)}, u32[]{:S(2)}, u32[]{:S(2)}) collective-permute-start(bf16[2,512,1536]{2,1,0:T(8,128)(2,1)S(1)} %slice.56.refs_0_), channel_id=1, source_target_pairs={{0,1},{1,2},{2,3},{4,5},{5,6},{6,7},{8,9},{9,10},{10,11},{12,13},{... | collective-permute-start | bytes 9437192 | tf_op jit(solution)/shard_map/ppermute | solution.py:243
  26.7 95.9 %collective-permute-start.8 = (bf16[2,256,1536]{2,1,0:T(8,128)(2,1)S(1)}, bf16[2,256,1536]{2,1,0:T(8,128)(2,1)S(1)}, u32[]{:S(2)}, u32[]{:S(2)}) collective-permute-start(bf16[2,256,1536]{2,1,0:T(8,128)(2,1)S(1)} %slice.57.refs_1_), channel_id=1, source_target_pairs={{1,0},{2,1},{3,2},{5,4},{6,5},{7,6},{9,8},{10,9},{11,10},{13,12},{... | collective-permute-start | bytes 4718600 | tf_op jit(solution)/shard_map/ppermute | solution.py:244
  28.0 95.9 %collective-permute-start.6 = (bf16[2,256,1536]{2,1,0:T(8,128)(2,1)S(1)}, bf16[2,256,1536]{2,1,0:T(8,128)(2,1)S(1)}, u32[]{:S(2)}, u32[]{:S(2)}) collective-permute-start(bf16[2,256,1536]{2,1,0:T(8,128)(2,1)S(1)} %slice.57.refs_1_), channel_id=1, source_target_pairs={{0,1},{1,2},{2,3},{4,5},{5,6},{6,7},{8,9},{9,10},{10,11},{12,13},{... | collective-permute-start | bytes 4718600 | tf_op jit(solution)/shard_map/ppermute | solution.py:243
  32.1 1.2 copy-start.3
  89.0 141.3 %collective-permute-start.4 = (bf16[2,512,1536]{2,1,0:T(8,128)(2,1)}, bf16[2,512,1536]{2,1,0:T(8,128)(2,1)}, u32[]{:S(2)}, u32[]{:S(2)}) collective-permute-start(bf16[2,512,1536]{2,1,0:T(8,128)(2,1)} %collective-permute-done.3.refs_6_.refs_1_), channel_id=1, source_target_pairs={{1,0},{2,1},{3,2},{5,4},{6,5},{7,6},{9,8},{10,9},{11,10},{13,12},{... | collective-permute-start | bytes 9437192 | tf_op jit(solution)/shard_map/ppermute | solution.py:244
  90.3 141.3 %collective-permute-start.1 = (bf16[2,512,1536]{2,1,0:T(8,128)(2,1)}, bf16[2,512,1536]{2,1,0:T(8,128)(2,1)}, u32[]{:S(2)}, u32[]{:S(2)}) collective-permute-start(bf16[2,512,1536]{2,1,0:T(8,128)(2,1)} %collective-permute-done.refs_2_), channel_id=1, source_target_pairs={{0,1},{1,2},{2,3},{4,5},{5,6},{6,7},{8,9},{9,10},{10,11},{12,13},{... | collective-permute-start | bytes 9437192 | tf_op jit(solution)/shard_map/ppermute | solution.py:243
  122.7 108.9 %copy-start.5 = (bf16[2,256,1536]{2,1,0:T(8,128)(2,1)}, bf16[2,256,1536]{2,1,0:T(8,128)(2,1)S(1)}, u32[]{:S(2)}) copy-start(bf16[2,256,1536]{2,1,0:T(8,128)(2,1)S(1)} %collective-permute-done.8.refs_7_.refs_1_) | copy-start | bytes 4718596
  122.7 101.1 %collective-permute-start.9 = (bf16[2,256,1536]{2,1,0:T(8,128)(2,1)S(1)}, bf16[2,256,1536]{2,1,0:T(8,128)(2,1)}, u32[]{:S(2)}, u32[]{:S(2)}) collective-permute-start(bf16[2,256,1536]{2,1,0:T(8,128)(2,1)S(1)} %collective-permute-done.8.refs_7_.refs_1_), channel_id=1, source_target_pairs={{1,0},{2,1},{3,2},{5,4},{6,5},{7,6},{9,8},{10,9},{11,10},{13,12},{... | collective-permute-start | bytes 4718600 | tf_op jit(solution)/shard_map/ppermute | solution.py:244
  124.0 101.1 %collective-permute-start.7 = (bf16[2,256,1536]{2,1,0:T(8,128)(2,1)S(1)}, bf16[2,256,1536]{2,1,0:T(8,128)(2,1)}, u32[]{:S(2)}, u32[]{:S(2)}) collective-permute-start(bf16[2,256,1536]{2,1,0:T(8,128)(2,1)S(1)} %collective-permute-done.6.refs_3_), channel_id=1, source_target_pairs={{0,1},{1,2},{2,3},{4,5},{5,6},{6,7},{8,9},{9,10},{10,11},{12,13},{... | collective-permute-start | bytes 4718600 | tf_op jit(solution)/shard_map/ppermute | solution.py:243
  129.1 1.1 copy-start.7
  223.8 72.6 %collective-permute-start.11 = (bf16[2,256,1536]{2,1,0:T(8,128)(2,1)}, bf16[2,256,1536]{2,1,0:T(8,128)(2,1)}, u32[]{:S(2)}, u32[]{:S(2)}) collective-permute-start(bf16[2,256,1536]{2,1,0:T(8,128)(2,1)} %collective-permute-done.9.refs_9_.refs_2_), channel_id=1, source_target_pairs={{1,0},{2,1},{3,2},{5,4},{6,5},{7,6},{9,8},{10,9},{11,10},{13,12},{... | collective-permute-start | bytes 4718600 | tf_op jit(solution)/shard_map/ppermute | solution.py:244
  225.1 71.4 %collective-permute-start.10 = (bf16[2,256,1536]{2,1,0:T(8,128)(2,1)}, bf16[2,256,1536]{2,1,0:T(8,128)(2,1)}, u32[]{:S(2)}, u32[]{:S(2)}) collective-permute-start(bf16[2,256,1536]{2,1,0:T(8,128)(2,1)} %collective-permute-done.7.refs_5_), channel_id=1, source_target_pairs={{0,1},{1,2},{2,3},{4,5},{5,6},{6,7},{8,9},{9,10},{10,11},{12,13},{... | collective-permute-start | bytes 4718600 | tf_op jit(solution)/shard_map/ppermute | solution.py:243
  230.3 97.8 %collective-permute-start.5 = (bf16[2,512,1536]{2,1,0:T(8,128)(2,1)}, bf16[2,512,1536]{2,1,0:T(8,128)(2,1)}, u32[]{:S(2)}, u32[]{:S(2)}) collective-permute-start(bf16[2,512,1536]{2,1,0:T(8,128)(2,1)} %collective-permute-done.4.refs_8_.refs_2_), channel_id=1, source_target_pairs={{1,0},{2,1},{3,2},{5,4},{6,5},{7,6},{9,8},{10,9},{11,10},{13,12},{... | collective-permute-start | bytes 9437192 | tf_op jit(solution)/shard_map/ppermute | solution.py:244
  231.6 97.4 %collective-permute-start.2 = (bf16[2,512,1536]{2,1,0:T(8,128)(2,1)}, bf16[2,512,1536]{2,1,0:T(8,128)(2,1)S(1)}, u32[]{:S(2)}, u32[]{:S(2)}) collective-permute-start(bf16[2,512,1536]{2,1,0:T(8,128)(2,1)} %collective-permute-done.1.refs_4_), channel_id=1, source_target_pairs={{0,1},{1,2},{2,3},{4,5},{5,6},{6,7},{8,9},{9,10},{10,11},{12,13},{... | collective-permute-start | bytes 9437192 | tf_op jit(solution)/shard_map/ppermute | solution.py:243
  235.8 1.4 copy-start.4
  237.2 1.4 copy-start.8
  238.6 57.8 %copy-start.6 = (bf16[2,256,1536]{2,1,0:T(8,128)(2,1)S(1)}, bf16[2,256,1536]{2,1,0:T(8,128)(2,1)}, u32[]{:S(2)}) copy-start(bf16[2,256,1536]{2,1,0:T(8,128)(2,1)} %copy-done.5) | copy-start | bytes 4718596
  348.8 7.5 %collective-permute-start.13 = (f32[3,1,24]{2,1,0:T(1,128)S(1)}, f32[3,1,24]{2,1,0:T(1,128)S(1)}, u32[]{:S(2)}, u32[]{:S(2)}) collective-permute-start(f32[3,1,24]{2,1,0:T(1,128)S(1)} %slice.73), channel_id=1, source_target_pairs={{4,0},{8,4},{12,8},{16,12},{20,16},{24,20},{28,24},{5,1},{9,5},{13... | collective-permute-start | bytes 872 | tf_op jit(solution)/shard_map/ppermute | solution.py:24
  353.4 3.6 collective-permute-start.12
  357.1 5.3 %collective-permute-start.14 = (f32[3,14,1]{2,1,0:T(8,128)S(1)}, f32[3,14,1]{2,1,0:T(8,128)S(1)}, u32[]{:S(2)}, u32[]{:S(2)}) collective-permute-start(f32[3,14,1]{2,1,0:T(8,128)S(1)} %get-tuple-element.13), channel_id=1, source_target_pairs={{0,1},{1,2},{2,3},{4,5},{5,6},{6,7},{8,9},{9,10},{10,11},{12,13},{... | collective-permute-start | bytes 512 | tf_op jit(solution)/shard_map/ppermute | solution.py:21
  361.1 5.4 %collective-permute-start.15 = (f32[3,14,1]{2,1,0:T(8,128)S(1)}, f32[3,14,1]{2,1,0:T(8,128)S(1)}, u32[]{:S(2)}, u32[]{:S(2)}) collective-permute-start(f32[3,14,1]{2,1,0:T(8,128)S(1)} %get-tuple-element.14), channel_id=1, source_target_pairs={{1,0},{2,1},{3,2},{5,4},{6,5},{7,6},{9,8},{10,9},{11,10},{13,12},{... | collective-permute-start | bytes 512 | tf_op jit(solution)/shard_map/ppermute | solution.py:24
  367.1 2.3 copy-start.1
Sparse Core Ops, SparseCore 0:
  15.0 182.0 all-gather.2

commit v3 on v2

--- a/solution.py
+++ b/solution.py
@@ -114,7 +114,7 @@
     depth, columns = panel.shape[2], panel.shape[3]
     parts = width // depth
     wide = largest(columns, (512, 384, 256, 128))
-    tile_rows = largest(rows, (256, 128, 64))
+    tile_rows = largest(rows, (256, 384, 192, 128, 64))
     tiles = rows // tile_rows
     phases = len(options)
     place = first_row // rows
@@ -228,16 +228,15 @@
     _, row_count, col_count = data.shape
     count = lax.axis_size("rcv")
     place = lax.axis_index("rcv")
-    panel = lax.all_gather(scale(data, source_term), "src", axis=0)
-
     block_rows = row_count // LINE
     block_cols = col_count // LINE
-    third = row_count // 3
-    edges = [0, 2 * third, row_count] if block_rows % 3 == 0 else [0, row_count]
+    half = row_count // 2
+    edges = [0, half, row_count] if block_rows % 2 == 0 else [0, row_count]
     spans = list(zip(edges[:-1], edges[1:]))
     upward = [(i, i + 1) for i in range(count - 1)]
     downward = [(i + 1, i) for i in range(count - 1)]
     own = [lax.slice_in_dim(data, low, high, axis=1) for low, high in spans]
+    panel = lax.all_gather(scale(data, source_term), "src", axis=0)
     ups, downs = [own], [own]
     for _ in range(count - 1):
         ups.append([lax.ppermute(piece, "rcv", upward) for piece in ups[-1]])
@@ -258,7 +257,7 @@
     total = multiply(blocks, options, block_of, choice_of, panel)
     end = count - 1
     multiples, sums_of = None, []
-    for index in reversed(range(len(spans))):
+    for index in range(len(spans)):
         multiples, row_sums = multiply(
             [[block[index]] for block in [ups[end]] + downs[1:]],
             [tuple(range(count))],
@@ -269,7 +268,7 @@
             (total, data, multiples),
         )
         lines = (spans[index][1] - spans[index][0]) // LINE
-        sums_of.insert(0, row_sums.transpose(1, 0, 2, 3).reshape(3, lines, block_cols, LINE).sum(axis=3))
+        sums_of.append(row_sums.transpose(1, 0, 2, 3).reshape(3, lines, block_cols, LINE).sum(axis=3))
 
     sums = with_halo(jnp.concatenate(sums_of, axis=1), (("src", 1), ("rcv", 2)), 1)
     window = jnp.zeros((3, block_rows, block_cols), jnp.float32)

time: 383 us -> 377 us (0.984)
  waiting for transfers between devices: 201 us -> 196 us
    ppermute x6, waiting for transfers between devices: 195 us -> 189 us  [on_device(): downs.append([lax.ppermute(piece, 'rcv', downward) for piece in downs[-1]])]
    unnamed x20 -> x18, local copies, waits for them, and re-layouts: 12 us -> 13.2 us
  transfers between devices with their start and end apart: 17 -> 17, of which waited for: 7 -> 8; matrix products, arithmetic and copies ran while one was open for 1% -> 1% of each run, Pallas kernels for 18% -> 19%
where the time goes in v3:
time: 377 us; the launch traced here: 374 us
  waiting for transfers between devices  196 us (52%)
  Pallas kernels  93.8 us (25%)
  starting transfers between devices  53 us (14%)
  local copies, waits for them, and re-layouts  17.4 us (5%)
  between operations  13.7 us (4%)
    ppermute x6, waiting for transfers between devices, on_device(): downs.append([lax.ppermute(piece, 'rcv', downward) for piece in downs[-1]])  189 us
    pallas_call x3, Pallas kernels, multiply(): pl.pallas_call(functools.partial(product_kernel, options, tile_rows, last...  86.9 us
    ppermute x6, starting transfers between devices, on_device(): ups.append([lax.ppermute(piece, 'rcv', upward) for piece in ups[-1]])  33.3 us
    unnamed x18, local copies, waits for them, and re-layouts  13.2 us
    ppermute x2, starting transfers between devices, with_halo(): lax.ppermute(lax.slice_in_dim(block, block.shape[dim] - width, None, axis...  8.81 us
    ppermute x6, starting transfers between devices, on_device(): downs.append([lax.ppermute(piece, 'rcv', downward) for piece in downs[-1]])  7.69 us
  transfers between devices with their start and end apart: 17, of which 8 were waited for; matrix products, arithmetic and copies ran while one was open for 1% of the time, Pallas kernels for 19%

profile of v3, /device:TPU:1, one launch (start us, length us, event | category | flops | bytes accessed | tf_op | source)
XLA Modules:
  0.0 374.4 jit_solution(7574636890960222344)
XLA Ops:
  6.5 1.0 copy.6.weight_ref
  7.5 2.3 copy-done
  9.9 2.8 shard_map.28
  12.7 2.2 copy-done.2
  14.9 2.7 fusion.4
  17.6 1.3 collective-permute-start.8
  18.9 6.1 %collective-permute-start.6 = (bf16[2,384,1536]{2,1,0:T(8,128)(2,1)S(1)}, bf16[2,384,1536]{2,1,0:T(8,128)(2,1)}, u32[]{:S(2)}, u32[]{:S(2)}) collective-permute-start(bf16[2,384,1536]{2,1,0:T(8,128)(2,1)S(1)} %get-tuple-element.13.refs_0_), channel_id=1, source_target_pairs={{0,1},{1,2},{2,3},{4,5},{5,6},{6,7},{8,9},{9,10},{10,11},{12,13},{... | collective-permute-start | bytes 7077896 | tf_op jit(solution)/shard_map/ppermute | solution.py:242
  25.0 1.6 copy-done.5
  26.5 1.3 collective-permute-start.3
  27.8 5.5 %collective-permute-start = (bf16[2,384,1536]{2,1,0:T(8,128)(2,1)S(1)}, bf16[2,384,1536]{2,1,0:T(8,128)(2,1)}, u32[]{:S(2)}, u32[]{:S(2)}) collective-permute-start(bf16[2,384,1536]{2,1,0:T(8,128)(2,1)S(1)} %get-tuple-element.14.refs_1_), channel_id=1, source_target_pairs={{0,1},{1,2},{2,3},{4,5},{5,6},{6,7},{8,9},{9,10},{10,11},{12,13},{... | collective-permute-start | bytes 7077896 | tf_op jit(solution)/shard_map/ppermute | solution.py:242
  33.4 1.4 copy-done.7
  34.8 37.9 %collective-permute-done.8.refs_6_.refs_1_ = bf16[2,384,1536]{2,1,0:T(8,128)(2,1)} collective-permute-done((bf16[2,384,1536]{2,1,0:T(8,128)(2,1)S(1)}, bf16[2,384,1536]{2,1,0:T(8,128)(2,1)}, u32[]{:S(2)}, u32[]{:S(2)}) %collective-permute-start.8) | collective-permute-done | bytes 2359328 | tf_op jit(solution)/shard_map/ppermute | solution.py:243
  72.7 1.3 collective-permute-start.9
  74.0 5.4 %collective-permute-start.7 = (bf16[2,384,1536]{2,1,0:T(8,128)(2,1)}, bf16[2,384,1536]{2,1,0:T(8,128)(2,1)}, u32[]{:S(2)}, u32[]{:S(2)}) collective-permute-start(bf16[2,384,1536]{2,1,0:T(8,128)(2,1)} %collective-permute-done.6.refs_2_), channel_id=1, source_target_pairs={{0,1},{1,2},{2,3},{4,5},{5,6},{6,7},{8,9},{9,10},{10,11},{12,13},{... | collective-permute-start | bytes 7077896 | tf_op jit(solution)/shard_map/ppermute | solution.py:242
  79.4 43.9 %collective-permute-done.3.refs_7_.refs_1_ = bf16[2,384,1536]{2,1,0:T(8,128)(2,1)S(1)} collective-permute-done((bf16[2,384,1536]{2,1,0:T(8,128)(2,1)S(1)}, bf16[2,384,1536]{2,1,0:T(8,128)(2,1)S(1)}, u32[]{:S(2)}, u32[]{:S(2)}) %collective-permute-start.3) | collective-permute-done | bytes 2359328 | tf_op jit(solution)/shard_map/ppermute | solution.py:243
  123.3 1.3 collective-permute-start.4
  124.6 5.5 %collective-permute-start.1 = (bf16[2,384,1536]{2,1,0:T(8,128)(2,1)}, bf16[2,384,1536]{2,1,0:T(8,128)(2,1)}, u32[]{:S(2)}, u32[]{:S(2)}) collective-permute-start(bf16[2,384,1536]{2,1,0:T(8,128)(2,1)} %collective-permute-done.refs_3_), channel_id=1, source_target_pairs={{0,1},{1,2},{2,3},{4,5},{5,6},{6,7},{8,9},{9,10},{10,11},{12,13},{... | collective-permute-start | bytes 7077896 | tf_op jit(solution)/shard_map/ppermute | solution.py:242
  130.1 0.1 pad_add_fusion
  130.1 43.7 %collective-permute-done.9.refs_8_.refs_2_ = bf16[2,384,1536]{2,1,0:T(8,128)(2,1)} collective-permute-done((bf16[2,384,1536]{2,1,0:T(8,128)(2,1)}, bf16[2,384,1536]{2,1,0:T(8,128)(2,1)}, u32[]{:S(2)}, u32[]{:S(2)}) %collective-permute-start.9) | collective-permute-done | bytes 2359328 | tf_op jit(solution)/shard_map/ppermute | solution.py:243
  173.8 1.3 collective-permute-start.11
  175.1 5.4 %collective-permute-start.10 = (bf16[2,384,1536]{2,1,0:T(8,128)(2,1)}, bf16[2,384,1536]{2,1,0:T(8,128)(2,1)}, u32[]{:S(2)}, u32[]{:S(2)}) collective-permute-start(bf16[2,384,1536]{2,1,0:T(8,128)(2,1)} %collective-permute-done.7.refs_4_), channel_id=1, source_target_pairs={{0,1},{1,2},{2,3},{4,5},{5,6},{6,7},{8,9},{9,10},{10,11},{12,13},{... | collective-permute-start | bytes 7077896 | tf_op jit(solution)/shard_map/ppermute | solution.py:242
  180.5 43.9 %collective-permute-done.4.refs_9_.refs_2_ = bf16[2,384,1536]{2,1,0:T(8,128)(2,1)} collective-permute-done((bf16[2,384,1536]{2,1,0:T(8,128)(2,1)S(1)}, bf16[2,384,1536]{2,1,0:T(8,128)(2,1)}, u32[]{:S(2)}, u32[]{:S(2)}) %collective-permute-start.4) | collective-permute-done | bytes 2359328 | tf_op jit(solution)/shard_map/ppermute | solution.py:243
  224.4 1.3 collective-permute-start.5
  225.7 5.4 %collective-permute-start.2 = (bf16[2,384,1536]{2,1,0:T(8,128)(2,1)}, bf16[2,384,1536]{2,1,0:T(8,128)(2,1)}, u32[]{:S(2)}, u32[]{:S(2)}) collective-permute-start(bf16[2,384,1536]{2,1,0:T(8,128)(2,1)} %collective-permute-done.1.refs_5_), channel_id=1, source_target_pairs={{0,1},{1,2},{2,3},{4,5},{5,6},{6,7},{8,9},{9,10},{10,11},{12,13},{... | collective-permute-start | bytes 7077896 | tf_op jit(solution)/shard_map/ppermute | solution.py:242
  231.1 1.7 copy-done.6
  232.8 1.7 copy-done.8
  234.4 56.0 %shard_map.29.refs_5_ = f32[2,768,1536]{2,1,0:T(8,128)} custom-call(s32[3]{0:T(128)S(1)} %get-tuple-element.19.block_of, s32[3]{0:T(128)S(1)} %get-tuple-element.20.choice_of, bf16[2,384,1536]{2,1,0:T(8,128)(2,1)S(1)} %copy-done.6, bf16[2,384,1536]{2,1,0:T(8,128)(2,1)S(1)} %copy-done.8, bf16[2,384,1536]{2,1,0:T(8,128)(2,1)} %collective-permute-done.6.refs_2_, ...), custom_call_target="tpu_custom_call" | custom-call | flops 43486543872 | bytes 42467328 | tf_op jit(solution)/shard_map/pallas_call | solution.py:150
  290.5 15.6 %shard_map.30 = (bf16[2,768,1536]{2,1,0:T(8,128)(2,1)}, f32[1,3,6,1536]{3,2,1,0:T(8,128)S(1)}) custom-call(s32[1]{0:T(128)} %bitcast.block_of, s32[1]{0:T(128)} %bitcast.1.choice_of, bf16[2,384,1536]{2,1,0:T(8,128)(2,1)} %collective-permute-done.10.refs_0_, bf16[2,384,1536]{2,1,0:T(8,128)(2,1)} %collective-permute-done.8.refs_6_.refs_1_, ...), custom_call_target="tpu_custom_call" | custom-call | flops 7247757312 | bytes 11796480 | tf_op jit(solution)/shard_map/pallas_call | solution.py:150
  306.0 19.4 %collective-permute-done.5.refs_3_ = bf16[2,384,1536]{2,1,0:T(8,128)(2,1)} collective-permute-done((bf16[2,384,1536]{2,1,0:T(8,128)(2,1)}, bf16[2,384,1536]{2,1,0:T(8,128)(2,1)}, u32[]{:S(2)}, u32[]{:S(2)}) %collective-permute-start.5) | collective-permute-done | bytes 2359328 | tf_op jit(solution)/shard_map/ppermute | solution.py:243
  325.5 0.9 collective-permute-done.2.refs_0_
  326.4 15.4 %shard_map.31 = (bf16[2,768,1536]{2,1,0:T(8,128)(2,1)}, f32[1,3,6,1536]{3,2,1,0:T(8,128)S(1)}) custom-call(s32[1]{0:T(128)} %bitcast.block_of, s32[1]{0:T(128)} %bitcast.1.choice_of, bf16[2,384,1536]{2,1,0:T(8,128)(2,1)} %collective-permute-done.2.refs_0_, bf16[2,384,1536]{2,1,0:T(8,128)(2,1)S(1)} %copy-done.4, ...), custom_call_target="tpu_custom_call", output_to_operand_aliasing={{0}: (9, {})} | custom-call | flops 7247757312 | bytes 11796480 | tf_op jit(solution)/shard_map/pallas_call | solution.py:150
  341.7 0.1 reshape_transpose.6
  341.8 0.1 reduce_sum.18
  342.0 4.7 %collective-permute-start.12 = (f32[3,1,24]{2,1,0:T(1,128)S(1)}, f32[3,1,24]{2,1,0:T(1,128)S(1)}, u32[]{:S(2)}, u32[]{:S(2)}) collective-permute-start(f32[3,1,24]{2,1,0:T(1,128)S(1)} %slice.72), channel_id=1, source_target_pairs={{0,4},{4,8},{8,12},{12,16},{16,20},{20,24},{24,28},{1,5},{5,9},{9,... | collective-permute-start | bytes 872 | tf_op jit(solution)/shard_map/ppermute | solution.py:21
  346.7 0.1 reshape_transpose.7
  346.8 0.1 reduce_sum.19
  347.0 1.9 collective-permute-start.13
  348.9 3.0 collective-permute-done.13
  351.9 0.1 fusion.5
  351.9 4.1 %collective-permute-start.14 = (f32[3,14,1]{2,1,0:T(8,128)S(1)}, f32[3,14,1]{2,1,0:T(8,128)S(1)}, u32[]{:S(2)}, u32[]{:S(2)}) collective-permute-start(f32[3,14,1]{2,1,0:T(8,128)S(1)} %get-tuple-element.17), channel_id=1, source_target_pairs={{0,1},{1,2},{2,3},{4,5},{5,6},{6,7},{8,9},{9,10},{10,11},{12,13},{... | collective-permute-start | bytes 512 | tf_op jit(solution)/shard_map/ppermute | solution.py:21
  356.1 1.3 collective-permute-start.15
  357.4 3.3 collective-permute-done.15
  360.6 0.1 maximum_maximum_fusion
  360.7 0.1 slice_add_fusion
  360.8 0.1 broadcast_in_dim.7
  361.0 0.2 reshape_reshape.3
  361.2 2.3 copy-done.1
  363.5 4.1 %shard_map.32 = bf16[2,768,1536]{2,1,0:T(8,128)(2,1)} custom-call(bf16[2,768,1536]{2,1,0:T(8,128)(2,1)S(1)} %copy-done.1, f32[6,2,2,1536]{3,2,1,0:T(2,128)S(1)} %bitcast.17), custom_call_target="tpu_custom_call" | custom-call | flops 7077888 | bytes 9437184 | tf_op jit(solution)/shard_map/pallas_call | solution.py:214
  (28 shorter events, 0.1 us)
Async XLA Ops:
  6.5 224.6 %all-gather.3.cloned.1.call-start = ((), (), s32[]{:S(2)}) async-start(), calls=%async_computation | async-start | bytes 42467328 | tf_op jit(solution)/shard_map/all_gather | solution.py:239
  7.5 2.3 copy-start
  12.7 2.2 copy-start.2
  17.6 55.1 %collective-permute-start.8 = (bf16[2,384,1536]{2,1,0:T(8,128)(2,1)S(1)}, bf16[2,384,1536]{2,1,0:T(8,128)(2,1)}, u32[]{:S(2)}, u32[]{:S(2)}) collective-permute-start(bf16[2,384,1536]{2,1,0:T(8,128)(2,1)S(1)} %get-tuple-element.13.refs_0_), channel_id=1, source_target_pairs={{1,0},{2,1},{3,2},{5,4},{6,5},{7,6},{9,8},{10,9},{11,10},{13,12},{... | collective-permute-start | bytes 7077896 | tf_op jit(solution)/shard_map/ppermute | solution.py:243
  18.9 55.1 %collective-permute-start.6 = (bf16[2,384,1536]{2,1,0:T(8,128)(2,1)S(1)}, bf16[2,384,1536]{2,1,0:T(8,128)(2,1)}, u32[]{:S(2)}, u32[]{:S(2)}) collective-permute-start(bf16[2,384,1536]{2,1,0:T(8,128)(2,1)S(1)} %get-tuple-element.13.refs_0_), channel_id=1, source_target_pairs={{0,1},{1,2},{2,3},{4,5},{5,6},{6,7},{8,9},{9,10},{10,11},{12,13},{... | collective-permute-start | bytes 7077896 | tf_op jit(solution)/shard_map/ppermute | solution.py:242
  25.0 1.6 copy-start.5
  26.5 96.7 %collective-permute-start.3 = (bf16[2,384,1536]{2,1,0:T(8,128)(2,1)S(1)}, bf16[2,384,1536]{2,1,0:T(8,128)(2,1)S(1)}, u32[]{:S(2)}, u32[]{:S(2)}) collective-permute-start(bf16[2,384,1536]{2,1,0:T(8,128)(2,1)S(1)} %get-tuple-element.14.refs_1_), channel_id=1, source_target_pairs={{1,0},{2,1},{3,2},{5,4},{6,5},{7,6},{9,8},{10,9},{11,10},{13,12},{... | collective-permute-start | bytes 7077896 | tf_op jit(solution)/shard_map/ppermute | solution.py:243
  27.8 96.7 %collective-permute-start = (bf16[2,384,1536]{2,1,0:T(8,128)(2,1)S(1)}, bf16[2,384,1536]{2,1,0:T(8,128)(2,1)}, u32[]{:S(2)}, u32[]{:S(2)}) collective-permute-start(bf16[2,384,1536]{2,1,0:T(8,128)(2,1)S(1)} %get-tuple-element.14.refs_1_), channel_id=1, source_target_pairs={{0,1},{1,2},{2,3},{4,5},{5,6},{6,7},{8,9},{9,10},{10,11},{12,13},{... | collective-permute-start | bytes 7077896 | tf_op jit(solution)/shard_map/ppermute | solution.py:242
  33.4 1.4 copy-start.7
  72.7 101.1 %collective-permute-start.9 = (bf16[2,384,1536]{2,1,0:T(8,128)(2,1)}, bf16[2,384,1536]{2,1,0:T(8,128)(2,1)}, u32[]{:S(2)}, u32[]{:S(2)}) collective-permute-start(bf16[2,384,1536]{2,1,0:T(8,128)(2,1)} %collective-permute-done.8.refs_6_.refs_1_), channel_id=1, source_target_pairs={{1,0},{2,1},{3,2},{5,4},{6,5},{7,6},{9,8},{10,9},{11,10},{13,12},{... | collective-permute-start | bytes 7077896 | tf_op jit(solution)/shard_map/ppermute | solution.py:243
  74.0 101.1 %collective-permute-start.7 = (bf16[2,384,1536]{2,1,0:T(8,128)(2,1)}, bf16[2,384,1536]{2,1,0:T(8,128)(2,1)}, u32[]{:S(2)}, u32[]{:S(2)}) collective-permute-start(bf16[2,384,1536]{2,1,0:T(8,128)(2,1)} %collective-permute-done.6.refs_2_), channel_id=1, source_target_pairs={{0,1},{1,2},{2,3},{4,5},{5,6},{6,7},{8,9},{9,10},{10,11},{12,13},{... | collective-permute-start | bytes 7077896 | tf_op jit(solution)/shard_map/ppermute | solution.py:242
  123.3 107.8 %copy-start.3 = (bf16[2,384,1536]{2,1,0:T(8,128)(2,1)}, bf16[2,384,1536]{2,1,0:T(8,128)(2,1)S(1)}, u32[]{:S(2)}) copy-start(bf16[2,384,1536]{2,1,0:T(8,128)(2,1)S(1)} %collective-permute-done.3.refs_7_.refs_1_) | copy-start | bytes 7077892
  123.3 101.1 %collective-permute-start.4 = (bf16[2,384,1536]{2,1,0:T(8,128)(2,1)S(1)}, bf16[2,384,1536]{2,1,0:T(8,128)(2,1)}, u32[]{:S(2)}, u32[]{:S(2)}) collective-permute-start(bf16[2,384,1536]{2,1,0:T(8,128)(2,1)S(1)} %collective-permute-done.3.refs_7_.refs_1_), channel_id=1, source_target_pairs={{1,0},{2,1},{3,2},{5,4},{6,5},{7,6},{9,8},{10,9},{11,10},{13,12},{... | collective-permute-start | bytes 7077896 | tf_op jit(solution)/shard_map/ppermute | solution.py:243
  124.6 101.1 %collective-permute-start.1 = (bf16[2,384,1536]{2,1,0:T(8,128)(2,1)}, bf16[2,384,1536]{2,1,0:T(8,128)(2,1)}, u32[]{:S(2)}, u32[]{:S(2)}) collective-permute-start(bf16[2,384,1536]{2,1,0:T(8,128)(2,1)} %collective-permute-done.refs_3_), channel_id=1, source_target_pairs={{0,1},{1,2},{2,3},{4,5},{5,6},{6,7},{8,9},{9,10},{10,11},{12,13},{... | collective-permute-start | bytes 7077896 | tf_op jit(solution)/shard_map/ppermute | solution.py:242
  173.8 116.6 %collective-permute-start.11 = (bf16[2,384,1536]{2,1,0:T(8,128)(2,1)}, bf16[2,384,1536]{2,1,0:T(8,128)(2,1)}, u32[]{:S(2)}, u32[]{:S(2)}) collective-permute-start(bf16[2,384,1536]{2,1,0:T(8,128)(2,1)} %collective-permute-done.9.refs_8_.refs_2_), channel_id=1, source_target_pairs={{1,0},{2,1},{3,2},{5,4},{6,5},{7,6},{9,8},{10,9},{11,10},{13,12},{... | collective-permute-start | bytes 7077896 | tf_op jit(solution)/shard_map/ppermute | solution.py:243
  175.1 115.3 %collective-permute-start.10 = (bf16[2,384,1536]{2,1,0:T(8,128)(2,1)}, bf16[2,384,1536]{2,1,0:T(8,128)(2,1)}, u32[]{:S(2)}, u32[]{:S(2)}) collective-permute-start(bf16[2,384,1536]{2,1,0:T(8,128)(2,1)} %collective-permute-done.7.refs_4_), channel_id=1, source_target_pairs={{0,1},{1,2},{2,3},{4,5},{5,6},{6,7},{8,9},{9,10},{10,11},{12,13},{... | collective-permute-start | bytes 7077896 | tf_op jit(solution)/shard_map/ppermute | solution.py:242
  224.4 101.1 %collective-permute-start.5 = (bf16[2,384,1536]{2,1,0:T(8,128)(2,1)}, bf16[2,384,1536]{2,1,0:T(8,128)(2,1)}, u32[]{:S(2)}, u32[]{:S(2)}) collective-permute-start(bf16[2,384,1536]{2,1,0:T(8,128)(2,1)} %collective-permute-done.4.refs_9_.refs_2_), channel_id=1, source_target_pairs={{1,0},{2,1},{3,2},{5,4},{6,5},{7,6},{9,8},{10,9},{11,10},{13,12},{... | collective-permute-start | bytes 7077896 | tf_op jit(solution)/shard_map/ppermute | solution.py:243
  225.7 100.7 %collective-permute-start.2 = (bf16[2,384,1536]{2,1,0:T(8,128)(2,1)}, bf16[2,384,1536]{2,1,0:T(8,128)(2,1)}, u32[]{:S(2)}, u32[]{:S(2)}) collective-permute-start(bf16[2,384,1536]{2,1,0:T(8,128)(2,1)} %collective-permute-done.1.refs_5_), channel_id=1, source_target_pairs={{0,1},{1,2},{2,3},{4,5},{5,6},{6,7},{8,9},{9,10},{10,11},{12,13},{... | collective-permute-start | bytes 7077896 | tf_op jit(solution)/shard_map/ppermute | solution.py:242
  231.1 1.7 copy-start.6
  232.8 1.7 copy-start.8
  290.5 35.9 %copy-start.4 = (bf16[2,384,1536]{2,1,0:T(8,128)(2,1)S(1)}, bf16[2,384,1536]{2,1,0:T(8,128)(2,1)}, u32[]{:S(2)}) copy-start(bf16[2,384,1536]{2,1,0:T(8,128)(2,1)} %copy-done.3) | copy-start | bytes 7077892
  342.0 6.9 %collective-permute-start.12 = (f32[3,1,24]{2,1,0:T(1,128)S(1)}, f32[3,1,24]{2,1,0:T(1,128)S(1)}, u32[]{:S(2)}, u32[]{:S(2)}) collective-permute-start(f32[3,1,24]{2,1,0:T(1,128)S(1)} %slice.72), channel_id=1, source_target_pairs={{0,4},{4,8},{8,12},{12,16},{16,20},{20,24},{24,28},{1,5},{5,9},{9,... | collective-permute-start | bytes 872 | tf_op jit(solution)/shard_map/ppermute | solution.py:21
  347.0 4.9 %collective-permute-start.13 = (f32[3,1,24]{2,1,0:T(1,128)S(1)}, f32[3,1,24]{2,1,0:T(1,128)S(1)}, u32[]{:S(2)}, u32[]{:S(2)}) collective-permute-start(f32[3,1,24]{2,1,0:T(1,128)S(1)} %slice.73), channel_id=1, source_target_pairs={{4,0},{8,4},{12,8},{16,12},{20,16},{24,20},{28,24},{5,1},{9,5},{13... | collective-permute-start | bytes 872 | tf_op jit(solution)/shard_map/ppermute | solution.py:24
  351.9 5.4 %collective-permute-start.14 = (f32[3,14,1]{2,1,0:T(8,128)S(1)}, f32[3,14,1]{2,1,0:T(8,128)S(1)}, u32[]{:S(2)}, u32[]{:S(2)}) collective-permute-start(f32[3,14,1]{2,1,0:T(8,128)S(1)} %get-tuple-element.17), channel_id=1, source_target_pairs={{0,1},{1,2},{2,3},{4,5},{5,6},{6,7},{8,9},{9,10},{10,11},{12,13},{... | collective-permute-start | bytes 512 | tf_op jit(solution)/shard_map/ppermute | solution.py:21
  356.1 4.6 %collective-permute-start.15 = (f32[3,14,1]{2,1,0:T(8,128)S(1)}, f32[3,14,1]{2,1,0:T(8,128)S(1)}, u32[]{:S(2)}, u32[]{:S(2)}) collective-permute-start(f32[3,14,1]{2,1,0:T(8,128)S(1)} %get-tuple-element.18), channel_id=1, source_target_pairs={{1,0},{2,1},{3,2},{5,4},{6,5},{7,6},{9,8},{10,9},{11,10},{13,12},{... | collective-permute-start | bytes 512 | tf_op jit(solution)/shard_map/ppermute | solution.py:24
  361.2 2.3 copy-start.1
Sparse Core Ops, SparseCore 0:
  15.0 182.0 all-gather.2
